TPU v7x, 32 devices: a whole 2x2x4 slice. The times are simulated.
32 devices in a mesh: sec: 2 (over x), ty: 4 (over y, core), tx: 4 (over z).
Axes of the slice: x: 2, y: 2, z: 4, core: 2. Of those that a mesh axis runs over, the one named last changes fastest.
Arguments:
- descriptors: bfloat16 [2, 4, 4, 1024, 128], P('sec', 'ty', 'tx'), may hold values from -4 to 4, as said below
- positions: bfloat16 [2, 4, 4, 2, 1024], P('sec', 'ty', 'tx'), may hold values from -1 to 1
- vertex_ids: int32 [2, 4, 4, 1024], P('sec', 'ty', 'tx'), may hold values from 0 to 262143, as said below
- candidate_blocks: int32 [2, 4, 4, 32], P('sec', 'ty', 'tx'), may hold values from 0 to 127, as said below
- candidate_count: int32 [2, 4, 4], P('sec', 'ty', 'tx'), may hold values from 8 to 32, as said below
- displacement: float32 [2, 2, 512, 512], P('sec', None, 'ty', 'tx'), may hold values from -3 to 3
- stiffness: float32 [2, 512, 512], P('sec', 'ty', 'tx'), may hold values from 0.25 to 4
Outputs:
- relaxed: float32 [2, 2, 512, 512], P('sec', None, 'ty', 'tx')
Inputs may be any that keep to these rules, and one draw needn't show every extreme that they name: `descriptors`: descriptor entries stay within the range. `candidate_blocks`: A list names distinct blocks tile * 8 + j of the next section; among its live entries at most 4 blocks come from any one tile, and some list has 4 live blocks of one tile. `candidate_count`: some tile has all 32 entries live. `vertex_ids`: ids follow the vertex numbering of the steps, anywhere in the section.
All inputs are finite; a program needn't handle non-finite values.
Results may differ from a plain program's by a relative error of at most 0.0019.
Values may be sent and summed in bfloat16 or wider, within the bound.
No kernel may reach another device: no remote copies, remote signals or barrier semaphores. Data moves between devices by JAX's collectives and lax.ppermute only.
A program may use at most 192 MiB of HBM per device.

v0:
```python
import functools
import math

import jax
import jax.numpy as jnp
from jax import lax
from jax.experimental import pallas as pl
from jax.experimental.pallas import tpu as pltpu
from jax.sharding import PartitionSpec as P

BLK = 128
ITERS = 4
LANES = 128
PLACE_ROWS = 16
GROUP = 2
BASE = 256
DIGITS = 3
VMEM_BYTES = 24 * 1024 * 1024

spring_sec = 0.5
spring_match = 1.0
relax_rate = 0.8


def passed_along(value, axis, by):
    devices = lax.axis_size(axis)
    pairs = [(i, i + by) for i in range(devices) if 0 <= i + by < devices]
    return lax.ppermute(value, axis, pairs)


def exchanged(value, axes):
    return lax.all_to_all(value, axes, split_axis=0, concat_axis=0, tiled=True)


def spread(value, axes):
    copies = jnp.broadcast_to(value[None], (lax.axis_size(axes),) + value.shape)
    return exchanged(copies, axes)


def nt_dot(a, b):
    return lax.dot_general(a, b, (((1,), (1,)), ((), ())), preferred_element_type=jnp.float32)


def in_vmem(count):
    return [pl.BlockSpec(memory_space=pltpu.VMEM)] * count


def in_smem():
    return pl.BlockSpec(memory_space=pltpu.SMEM)


def match_kernel(scale, key_tiles, work_ref, query_ref, *refs):
    key_refs = refs[:key_tiles]
    out_ref, key_buf, place_buf, state_buf, list_buf = refs[key_tiles:]
    shares, tile_rows = out_ref.shape[:2]
    point_total = state_buf.shape[2]
    rows = point_total // LANES // shares
    key_rows = key_buf.shape[1]
    part = key_rows // BLK
    total = key_tiles * part
    cand = work_ref.shape[0] // tile_rows

    number = 0
    for tile in range(tile_rows):
        for i in range(cand):
            place = work_ref[tile * cand + i]
            list_buf[number] = tile * total + place
            number = number + jnp.where(place >= 0, 1, 0)
        list_buf[number] = -1
        number = number + lax.rem(number, 2)
    for i in range(2 * GROUP):
        list_buf[number + i] = -1
    groups = lax.div(number + 2 * GROUP - 1, 2 * GROUP)

    row_at = lax.broadcasted_iota(jnp.int32, (PLACE_ROWS, LANES), 0)
    ids = []
    for tile, key_ref in enumerate(key_refs):
        key_buf[tile] = key_ref[pl.ds(0, key_rows), :]
        rest = key_ref[pl.ds(key_rows, key_ref.shape[0] - key_rows), :].astype(jnp.float32)
        for j in range(part):
            x, y = rest[j : j + 1, :], rest[part + j : part + j + 1, :]
            stacked = jnp.where(
                row_at == 0, x, jnp.where(row_at == 1, y, jnp.where(row_at == 2, 1.0, 0.0))
            )
            place_buf[tile * part + j] = stacked.astype(jnp.bfloat16)
        digits = [rest[2 * part + i * rows : 2 * part + (i + 1) * rows] for i in range(DIGITS)]
        ids.append(sum(digit * float(BASE**i) for i, digit in enumerate(digits)))

    state_row = lax.broadcasted_iota(jnp.int32, state_buf.shape[1:], 0)
    for tile in range(tile_rows):
        state_buf[tile] = jnp.where(state_row == 3, -1e30, 0.0)

    def item(at):
        codes = [list_buf[2 * at + i] for i in range(2)]
        tile = lax.div(jnp.maximum(codes[0], 0), total)
        keys, places = [], []
        for code in codes:
            block = lax.rem(jnp.maximum(code, 0), total)
            start = pl.multiple_of(lax.rem(block, part) * BLK, BLK)
            keys.append(key_buf[lax.div(block, part), pl.ds(start, BLK), :])
            kept = jnp.where(code >= 0, 1.0, 0.0).astype(jnp.bfloat16)
            places.append(place_buf[block] * kept)
        return tile, codes[0] >= 0, jnp.concatenate(keys, axis=0), jnp.concatenate(places, axis=1)

    @pl.loop(0, groups)
    def _(group):
        items = [item(group * GROUP + i) for i in range(GROUP)]
        scores = [
            nt_dot(keys, query_ref[tile, pl.ds(0, point_total), :]) * scale
            for tile, _, keys, _ in items
        ]
        tops = [jnp.max(score, axis=0, keepdims=True) for score in scores]
        weights = [jnp.exp2(s - top).astype(jnp.bfloat16) for s, top in zip(scores, tops)]
        sums = [
            jnp.dot(place, weight, preferred_element_type=jnp.float32)[0:8]
            for (_, _, _, place), weight in zip(items, weights)
        ]
        for (tile, live, _, _), top, added in zip(items, tops, sums):
            top = jnp.where(live, top, -1e30)
            state = state_buf[tile]
            before = state[3:4, :]
            both = jnp.maximum(before, top)
            state = state * jnp.exp2(before - both) + added * jnp.exp2(top - both)
            state_buf[tile] = jnp.where(state_row == 3, both, state)

    for tile in range(tile_rows):
        for row in range(shares * rows):
            lanes = pl.ds(row * LANES, LANES)
            for place, held in enumerate((3, 2, 0, 1)):
                out_ref[row // rows, tile, pl.ds(place * rows + row % rows, 1), :] = state_buf[
                    tile, pl.ds(held, 1), lanes
                ]
        for share in range(shares):
            out_ref[share, tile, pl.ds(4 * rows, key_tiles * rows), :] = jnp.concatenate(ids, axis=0)


def match(work, queries, keys, score_factor, shares, point_total, part):
    tile_rows, key_tiles = queries.shape[0], len(keys)
    width = queries.shape[2]
    rows = point_total // LANES // shares
    return pl.pallas_call(
        functools.partial(match_kernel, score_factor * math.log2(math.e), key_tiles),
        out_shape=jax.ShapeDtypeStruct(
            (shares, tile_rows, (4 + key_tiles) * rows, LANES), jnp.float32
        ),
        in_specs=[in_smem()] + in_vmem(1 + key_tiles),
        out_specs=pl.BlockSpec(memory_space=pltpu.VMEM),
        scratch_shapes=[
            pltpu.VMEM((key_tiles, part * BLK, width), jnp.bfloat16),
            pltpu.VMEM((key_tiles * part, PLACE_ROWS, LANES), jnp.bfloat16),
            pltpu.VMEM((tile_rows, 8, point_total), jnp.float32),
            pltpu.SMEM((work.shape[0] + 2 * GROUP + tile_rows,), jnp.int32),
        ],
        compiler_params=pltpu.CompilerParams(vmem_limit_bytes=VMEM_BYTES),
        cost_estimate=pl.CostEstimate(
            flops=tile_rows * key_tiles * part * point_total * BLK * width,
            bytes_accessed=2 * (queries.size + key_tiles * keys[0].size),
            transcendentals=tile_rows * key_tiles * part * point_total * BLK // 4,
        ),
        name="match",
    )(work, queries, *keys)


def combine_kernel(parts_ref, place_ref, out_ref):
    parts = parts_ref.shape[0]
    rows = place_ref.shape[0] // 2
    tops = [parts_ref[i, 0:rows, :] for i in range(parts)]
    top = functools.reduce(jnp.maximum, tops)
    total = x = y = jnp.zeros_like(top)
    for i in range(parts):
        gain = jnp.exp2(tops[i] - top)
        total += gain * parts_ref[i, rows : 2 * rows, :]
        x += gain * parts_ref[i, 2 * rows : 3 * rows, :]
        y += gain * parts_ref[i, 3 * rows : 4 * rows, :]
    pull = jnp.concatenate([x / total, y / total], axis=0) - place_ref[...].astype(jnp.float32)
    for i in range(out_ref.shape[0]):
        out_ref[i] = pull


def combine(parts, place, copies):
    return pl.pallas_call(
        combine_kernel,
        out_shape=jax.ShapeDtypeStruct((copies,) + place.shape, jnp.float32),
        in_specs=in_vmem(2),
        out_specs=pl.BlockSpec(memory_space=pltpu.VMEM),
        compiler_params=pltpu.CompilerParams(vmem_limit_bytes=VMEM_BYTES),
        name="combine",
    )(parts, place)


def one_hot(at, length, limits):
    count = at.shape[1]
    parts, done = [], 0
    for low, high in limits:
        spot = lax.broadcasted_iota(jnp.int32, (high - low, count), 0) + low
        if low > done:
            parts.append(jnp.zeros((low - done, count), jnp.bfloat16))
        parts.append(jnp.where(spot == at, 1.0, 0.0).astype(jnp.bfloat16))
        done = high
    if length > done:
        parts.append(jnp.zeros((length - done, count), jnp.bfloat16))
    return jnp.concatenate(parts, axis=0)


def flat(value):
    return jnp.concatenate([value[i : i + 1, :] for i in range(value.shape[0])], axis=1)


def hits(side, halo, tall, wide, row, col):
    up = lambda n: -(-n // 16) * 16
    limits = ((0, up(side + halo)), (wide - up(halo), wide))
    return one_hot(flat(row), tall, ((0, tall),)), one_hot(flat(col), wide, limits)


def spots_kernel(
    side, halo, key_tiles, at_ref, parts_ref, rounds_ref, spot_ref, count_ref, hit_buf
):
    shares, tile_rows, _, _ = parts_ref.shape
    rows = hit_buf.shape[2] // shares
    tall, wide = count_ref.shape

    def folded(at, length):
        return jnp.where(
            (at >= 0) & (at < side + halo), at, jnp.where((at < 0) & (at >= -halo), at + length, -1)
        )

    number = jnp.zeros(hit_buf.shape[2:], jnp.int32)
    tiles = [(i, j) for i in range(tile_rows) for j in range(key_tiles)]
    for at, (i, j) in enumerate(tiles):
        ids = jnp.concatenate(
            [parts_ref[k, i, pl.ds((4 + j) * rows, rows), :] for k in range(shares)], axis=0
        ).astype(jnp.int32)
        tile_of = lax.div(ids, side * side)
        within = lax.rem(ids, side * side)
        row = lax.div(tile_of, key_tiles) * side + lax.div(within, side) - at_ref[0]
        col = lax.rem(tile_of, key_tiles) * side + lax.rem(within, side) - at_ref[1]
        row, col = folded(row, side + 2 * halo), folded(col, wide)
        here = (row >= 0) & (col >= 0)
        hit_buf[0, at] = jnp.where(here, number, -1)
        hit_buf[1, at] = row
        hit_buf[2, at] = col
        number = number + here.astype(jnp.int32)
    rounds = jnp.max(number)
    rounds_ref[0] = rounds
    count_ref[...] = jnp.zeros_like(count_ref)

    @pl.loop(0, rounds)
    def _(k):
        tile_of = row = col = jnp.full(number.shape, -1, jnp.int32)
        for at, (i, j) in enumerate(tiles):
            here = hit_buf[0, at] == k
            tile_of = jnp.where(here, i * key_tiles + at_ref[3 + j], tile_of)
            row = jnp.where(here, hit_buf[1, at], row)
            col = jnp.where(here, hit_buf[2, at], col)
        spot_ref[k, 0] = tile_of
        spot_ref[k, 1] = row
        spot_ref[k, 2] = col
        row_hit, col_hit = hits(side, halo, tall, wide, row, col)
        count_ref[...] += nt_dot(row_hit, col_hit)


def spots(side, halo, key_tiles, wide, at, parts, rows):
    tall = -(-(side + 2 * halo) // 16) * 16
    points = (parts.shape[0] * rows, LANES)
    tiles = parts.shape[1] * key_tiles
    return pl.pallas_call(
        functools.partial(spots_kernel, side, halo, key_tiles),
        out_shape=(
            jax.ShapeDtypeStruct((1,), jnp.int32),
            jax.ShapeDtypeStruct((tiles, 3) + points, jnp.int32),
            jax.ShapeDtypeStruct((tall, wide), jnp.float32),
        ),
        in_specs=[in_smem()] + in_vmem(1),
        out_specs=(in_smem(),) + (pl.BlockSpec(memory_space=pltpu.VMEM),) * 2,
        scratch_shapes=[pltpu.VMEM((3, tiles) + points, jnp.int32)],
        compiler_params=pltpu.CompilerParams(vmem_limit_bytes=VMEM_BYTES),
        cost_estimate=pl.CostEstimate(
            flops=10 * tall * points[0] * LANES * wide,
            bytes_accessed=8 * parts.size,
            transcendentals=0,
        ),
        name="spots",
    )(at, parts)


def vertex_sums(side, halo, rounds_ref, spot_ref, points_ref, sum_ref):
    _, tall, wide = sum_ref.shape
    shares, tiles, both_rows, _ = points_ref.shape
    rows = both_rows // 2
    sum_ref[...] = jnp.zeros_like(sum_ref)

    @pl.loop(0, rounds_ref[0])
    def _(k):
        tile_of = spot_ref[k, 0]
        x = y = jnp.zeros(tile_of.shape, jnp.float32)
        for tile in range(tiles):
            here = tile_of == tile
            values = [points_ref[share, tile] for share in range(shares)]
            x = jnp.where(here, jnp.concatenate([v[:rows] for v in values], axis=0), x)
            y = jnp.where(here, jnp.concatenate([v[rows:] for v in values], axis=0), y)
        row_hit, col_hit = hits(side, halo, tall, wide, spot_ref[k, 1], spot_ref[k, 2])
        parts = []
        for value in (flat(x), flat(y)):
            high = value.astype(jnp.bfloat16)
            low = (value - high.astype(jnp.float32)).astype(jnp.bfloat16)
            parts += [row_hit * high, row_hit * low]
        summed = nt_dot(jnp.concatenate(parts, axis=0), col_hit)
        sum_ref[0] += summed[0:tall] + summed[tall : 2 * tall]
        sum_ref[1] += summed[2 * tall : 3 * tall] + summed[3 * tall :]


def sums_kernel(side, halo, rounds_ref, spot_ref, points_ref, out_ref, sum_ref):
    vertex_sums(side, halo, rounds_ref, spot_ref, points_ref, sum_ref)
    out_ref[...] = sum_ref[:, pl.ds(0, out_ref.shape[1]), :]


def relax_kernel(
    side,
    halo,
    extent,
    at_ref,
    rounds_ref,
    spot_ref,
    count_ref,
    points_ref,
    mesh_ref,
    out_ref,
    sum_ref,
):
    vertex_sums(side, halo, rounds_ref, spot_ref, points_ref, sum_ref)
    span = side + 2 * halo
    wide = sum_ref.shape[2]
    shape = (span, wide)
    row = lax.broadcasted_iota(jnp.int32, shape, 0)
    col = lax.broadcasted_iota(jnp.int32, shape, 1)
    row = jnp.where(row < side + halo, row, row - span) + at_ref[0]
    col = jnp.where(col < side + halo, col, col - wide) + at_ref[1]
    inside = (row >= 0) & (row < extent[0]) & (col >= 0) & (col < extent[1])
    own_pulled = (at_ref[2] == 0).astype(jnp.float32)
    linked = 1.0
    matched = count_ref[pl.ds(0, span), :]
    moving, gains, has, step = [], [], [], []
    for part, pulled in enumerate((own_pulled, 1.0 - own_pulled)):
        gain = mesh_ref[part * 3 + 2]
        diagonal = 4.0 * gain + spring_sec * linked + spring_match * matched * pulled
        gains.append(gain)
        has.append(matched * pulled)
        step.append(jnp.where(inside, relax_rate / diagonal, 0.0))
        moving.append(
            [(mesh_ref[part * 3 + c], sum_ref[c, pl.ds(0, span), :] * pulled) for c in range(2)]
        )
    for sweep in range(ITERS):
        later = []
        for part in range(2):
            row_of = []
            for c in range(2):
                u, pulled = moving[part][c]
                other = moving[1 - part][c][0]
                laplace = (
                    pltpu.roll(u, 1, 0)
                    + pltpu.roll(u, span - 1, 0)
                    + pltpu.roll(u, 1, 1)
                    + pltpu.roll(u, wide - 1, 1)
                    - 4.0 * u
                )
                force = (
                    gains[part] * laplace
                    + spring_sec * (other - linked * u)
                    + spring_match * (pulled - has[part] * u)
                )
                row_of.append((u + step[part] * force, pulled))
            later.append(row_of)
        moving = later
    for c in range(2):
        out_ref[c] = moving[0][c][0][0:side, 0:side]


def with_halo(value, halo, wide):
    side = value.shape[1]
    after = passed_along(value[:, :halo], "ty", -1)
    before = passed_along(value[:, side - halo :], "ty", 1)
    value = jnp.concatenate([value, after, before], axis=1)
    after = passed_along(value[:, :, :halo].swapaxes(1, 2), "tx", -1).swapaxes(1, 2)
    before = passed_along(value[:, :, side - halo :].swapaxes(1, 2), "tx", 1).swapaxes(1, 2)
    gap = jnp.zeros(value.shape[:2] + (wide - side - 2 * halo,), value.dtype)
    return jnp.concatenate([value, after, gap, before], axis=2)


def sweeps(moving, gains, sums, number, at, side, halo, extent):
    sections = lax.axis_size("sec")
    sec_index = at[2]
    has_next = (sec_index < sections - 1).astype(jnp.float32)
    linked = (sec_index > 0).astype(jnp.float32) + has_next
    pulled, matched = sums * has_next, number * has_next
    span, wide = moving.shape[1:]
    row = jnp.arange(span)[:, None]
    col = jnp.arange(wide)[None, :]
    row = jnp.where(row < side + halo, row, row - span) + at[0]
    col = jnp.where(col < side + halo, col, col - wide) + at[1]
    inside = (row >= 0) & (row < extent[0]) & (col >= 0) & (col < extent[1])
    diagonal = 4.0 * gains + spring_sec * linked + spring_match * matched
    step = jnp.where(inside, relax_rate / jnp.where(inside, diagonal, 1.0), 0.0)
    for sweep in range(ITERS):
        lower_sec = passed_along(moving, "sec", 1)
        upper_sec = passed_along(moving, "sec", -1)
        laplace = (
            jnp.roll(moving, 1, 1)
            + jnp.roll(moving, -1, 1)
            + jnp.roll(moving, 1, 2)
            + jnp.roll(moving, -1, 2)
            - 4.0 * moving
        )
        force = (
            gains * laplace
            + spring_sec * (lower_sec + upper_sec - linked * moving)
            + spring_match * (pulled - matched * moving)
        )
        moving = moving + step * force
    return moving[:, :side, :side]


def pack_kernel(desc_hbm, place_ref, ids_ref, list_ref, out_ref, sem):
    points = desc_hbm.shape[0]
    copy = pltpu.make_async_copy(desc_hbm, out_ref.at[pl.ds(0, points), :], sem)
    copy.start()

    def digit(value, i):
        return ((value >> (i * BASE.bit_length() - i)) & (BASE - 1)).astype(jnp.float32)

    def cut(row):
        return [row[:, i : i + LANES] for i in range(0, row.shape[1], LANES)]

    place, ids, listed = place_ref[...].astype(jnp.float32), ids_ref[...], list_ref[...]
    rows = cut(place[0:1]) + cut(place[1:2])
    for i in range(DIGITS):
        rows += cut(digit(ids, i))
    last = [digit(listed, 0), digit(listed, 1)]
    count = out_ref.shape[0] - points
    gap = jnp.zeros((count - len(rows) - PLACE_ROWS, LANES), jnp.float32)
    end = jnp.zeros((PLACE_ROWS - len(last), LANES), jnp.float32)
    rows += ([gap] if gap.shape[0] else []) + last + [end]
    out_ref[pl.ds(points, count), :] = jnp.concatenate(rows, axis=0).astype(jnp.bfloat16)
    copy.wait()


def pack(desc, place, ids, listed):
    per_tile = ids.shape[1] // LANES
    rows = -(-(2 + DIGITS) * per_tile // 16) * 16 + PLACE_ROWS
    return pl.pallas_call(
        pack_kernel,
        out_shape=jax.ShapeDtypeStruct((desc.shape[0] + rows, LANES), jnp.bfloat16),
        in_specs=[pl.BlockSpec(memory_space=pl.ANY)] + in_vmem(3),
        out_specs=pl.BlockSpec(memory_space=pltpu.VMEM),
        scratch_shapes=[pltpu.SemaphoreType.DMA],
        compiler_params=pltpu.CompilerParams(vmem_limit_bytes=VMEM_BYTES),
        name="pack",
    )(desc, place, ids, listed)


def gathered(value, axis):
    devices, here = lax.axis_size(axis), lax.axis_index(axis)
    if devices & (devices - 1):
        partners = [[(i, (i + j) % devices) for i in range(devices)] for j in range(1, devices)]
        place = jnp.mod(here - jnp.arange(devices), devices)
    else:
        partners = [[(i, i ^ j) for i in range(devices)] for j in range(1, devices)]
        place = here ^ jnp.arange(devices)
    return [value] + [lax.ppermute(value, axis, pairs) for pairs in partners], place


def per_device(
    descriptors, positions, vertex_ids, candidate_blocks, candidate_count, displacement, stiffness
):
    point_total, width = descriptors.shape[3:]
    per_tile = point_total // BLK
    tile_rows, tile_cols = lax.axis_size("ty"), lax.axis_size("tx")
    sections = lax.axis_size("sec")
    sec_index = lax.axis_index("sec")
    tiles = tile_rows * tile_cols
    side = displacement.shape[3]
    halo = ITERS
    span = side + 2 * halo
    wide = -(-span // LANES) * LANES
    cand = candidate_blocks.shape[3]
    shares = 2 if sections == 2 and per_tile % 2 == 0 else 1
    part = per_tile // shares
    key_rows = part * BLK

    listed = jnp.concatenate([candidate_blocks[0, 0, 0], candidate_count[0, 0, 0][None]])
    listed = jnp.pad(listed, (0, LANES - cand - 1))[None]
    own = pack(descriptors[0, 0, 0], positions[0, 0, 0], vertex_ids[0, 0], listed)
    own_mesh = jnp.concatenate([displacement[0], stiffness], axis=0)
    swap = [(i, 1 - i) for i in range(2)]

    def of_share(rows):
        rows = rows.reshape(-1, shares, part, LANES)
        if shares == 2:
            rows = jnp.where(sec_index == 0, rows[:, 0], rows[:, 1])
        return rows.reshape(-1, LANES)

    if shares == 2:
        first = sec_index == 0
        share = sec_index
        other = lax.ppermute(own, "sec", swap)
        query = jnp.where(first, own, other)
        key = jnp.where(first, other[:key_rows], own[key_rows:point_total])
        key_place = jnp.where(
            first,
            other[point_total : point_total + 2 * per_tile],
            own[point_total : point_total + 2 * per_tile],
        )
    else:
        share = 0
        query = passed_along(own, "sec", 1)
        key, key_place = own[:point_total], own[point_total : point_total + 2 * per_tile]
    rest = query[point_total:]
    place = of_share(rest[: 2 * per_tile])
    ids = of_share(rest[2 * per_tile : (2 + DIGITS) * per_tile])
    filler = jnp.zeros((-(2 + DIGITS) * part % 16, LANES), jnp.bfloat16)
    key = jnp.concatenate([key, of_share(key_place), ids, filler], axis=0)
    query = jnp.concatenate([query[:point_total], rest[-PLACE_ROWS:]], axis=0)

    keys, key_col = gathered(key, "tx")
    queries = spread(query, "ty")

    lists = queries[:, point_total : point_total + 2].astype(jnp.int32)
    lists = lists[:, 0] + BASE * lists[:, 1]
    blocks, counts = lists[:, :cand], lists[:, cand : cand + 1]
    tile_of, within = blocks // per_tile, blocks % per_tile
    slot_of = jnp.zeros_like(tile_of)
    for i in range(tile_cols):
        slot_of = jnp.where(tile_of % tile_cols == key_col[i], i, slot_of)
    here = (
        (jnp.arange(cand)[None, :] < counts)
        & (tile_of // tile_cols == lax.axis_index("ty"))
        & (within // part == share)
    )
    work = jnp.where(here, slot_of * part + within % part, -1).reshape(-1).astype(jnp.int32)
    at = jnp.concatenate(
        [
            jnp.stack([lax.axis_index("ty") * side, lax.axis_index("tx") * side, sec_index]),
            key_col,
        ]
    ).astype(jnp.int32)
    extent = (side * tile_rows, side * tile_cols)
    sum_shape = pltpu.VMEM((2, -(-span // 16) * 16, wide), jnp.float32)

    if shares == 2:
        tied, keys[1] = lax.optimization_barrier((own_mesh, keys[1]))
        own_mesh = jnp.concatenate([own_mesh, lax.ppermute(tied, "sec", swap)], axis=0)
    parts = match(work, queries, keys, 16.0 / width, shares, point_total, part)
    own_mesh, parts = lax.optimization_barrier((own_mesh, parts))
    mesh_values = with_halo(own_mesh, halo, wide)
    if shares == 2:
        shape = parts.shape
        parts = exchanged(parts.reshape((-1,) + shape[2:]), ("sec", "ty"))
        points = exchanged(combine(parts, place, 2 * tiles), ("sec", "ty", "tx"))
        rounds, spot, number = spots(side, halo, tile_cols, wide, at, parts.reshape(shape), part)
        relaxed = pl.pallas_call(
            functools.partial(relax_kernel, side, halo, extent),
            out_shape=jax.ShapeDtypeStruct((2, side, side), jnp.float32),
            in_specs=[in_smem()] * 2 + in_vmem(4),
            out_specs=pl.BlockSpec(memory_space=pltpu.VMEM),
            scratch_shapes=[sum_shape],
            compiler_params=pltpu.CompilerParams(vmem_limit_bytes=VMEM_BYTES),
            name="relax",
        )(at, rounds, spot, number, points.reshape(2, tiles, -1, LANES), mesh_values)
        return relaxed[None]

    parts = exchanged(parts[0], "ty")
    points = passed_along(exchanged(combine(parts, place, tiles), ("ty", "tx")), "sec", -1)
    parts = passed_along(parts, "sec", -1)
    rounds, spot, number = spots(side, halo, tile_cols, wide, at, parts[None], part)
    sums = pl.pallas_call(
        functools.partial(sums_kernel, side, halo),
        out_shape=jax.ShapeDtypeStruct((2, span, wide), jnp.float32),
        in_specs=[in_smem()] + in_vmem(2),
        out_specs=pl.BlockSpec(memory_space=pltpu.VMEM),
        scratch_shapes=[sum_shape],
        compiler_params=pltpu.CompilerParams(vmem_limit_bytes=VMEM_BYTES),
        name="sums",
    )(rounds, spot, points[None])
    moving, gains = mesh_values[0:2], mesh_values[2]
    return sweeps(moving, gains, sums, number[:span], at, side, halo, extent)[None]


def solution(mesh):
    in_specs = (
        P("sec", "ty", "tx", None, None),
        P("sec", "ty", "tx", None, None),
        P("sec", "ty", "tx", None),
        P("sec", "ty", "tx", None),
        P("sec", "ty", "tx"),
        P("sec", None, "ty", "tx"),
        P("sec", "ty", "tx"),
    )
    out_specs = P("sec", None, "ty", "tx")
    return jax.shard_map(
        per_device, mesh=mesh, in_specs=in_specs, out_specs=out_specs, check_vma=False
    )
```

profile of v0, /device:TPU:0, one launch (start us, length us, event | category | flops | bytes accessed | tf_op | source)
XLA Modules:
  0.0 82.6 jit_solution(11574266651890796685)
XLA Ops:
  0.7 0.7 pad_add_fusion.1
  1.4 0.9 %copy-done = bf16[1,1,1,1024,128]{4,3,2,1,0:T(8,128)(2,1)S(1)} copy-done((bf16[1,1,1,1024,128]{4,3,2,1,0:T(8,128)(2,1)S(1)}, bf16[1,1,1,1024,128]{4,3,2,1,0:T(8,128)(2,1)}, u32[]{:S(2)}) %copy-start) | copy-done | bytes 262168
  2.3 0.7 copy-done.1
  3.0 0.7 copy-done.2
  3.8 3.0 %collective-permute-start = (bf16[1088,128]{1,0:T(8,128)(2,1)S(1)}, bf16[1088,128]{1,0:T(8,128)(2,1)S(1)}, u32[]{:S(2)}, u32[]{:S(2)}) collective-permute-start(bf16[1088,128]{1,0:T(8,128)(2,1)S(1)} %pack.1), channel_id=1, source_target_pairs={{0,16},{16,0},{1,17},{17,1},{2,18},{18,2},{3,19},{19,3},{4,20},{20... | collective-permute-start | bytes 835592 | tf_op jit(solution)/shard_map/ppermute | solution.py:504
  6.9 6.6 %collective-permute-done = bf16[1088,128]{1,0:T(8,128)(2,1)S(1)} collective-permute-done((bf16[1088,128]{1,0:T(8,128)(2,1)S(1)}, bf16[1088,128]{1,0:T(8,128)(2,1)S(1)}, u32[]{:S(2)}, u32[]{:S(2)}) %collective-permute-start) | collective-permute-done | bytes 278560 | tf_op jit(solution)/shard_map/ppermute | solution.py:504
  13.6 1.1 %broadcast_in_dim.29 = bf16[4,1040,128]{2,1,0:T(8,128)(2,1)} broadcast(bf16[1040,128]{1,0:T(8,128)(2,1)S(1)} %pad_maximum_fusion.3), dimensions={1,2} | broadcast | bytes 1331200 | tf_op jit(solution)/shard_map/broadcast_in_dim | solution.py:36
  14.7 3.6 %all-to-all-start = ((bf16[4,1040,128]{2,1,0:T(8,128)(2,1)}), bf16[4,1040,128]{2,1,0:T(8,128)(2,1)S(1)}, u32[]{:S(2)}, u32[]{:S(2)}) async-start(bf16[4,1040,128]{2,1,0:T(8,128)(2,1)} %broadcast_in_dim.29), calls=%async_computation | async-start | bytes 2129920 | tf_op jit(solution)/shard_map/all_to_all | solution.py:32
  18.6 1.9 %collective-permute-start.1 = (bf16[544,128]{1,0:T(8,128)(2,1)S(1)}, bf16[544,128]{1,0:T(8,128)(2,1)S(1)}, u32[]{:S(2)}, u32[]{:S(2)}) collective-permute-start(bf16[544,128]{1,0:T(8,128)(2,1)S(1)} %maximum_maximum_fusion.refs_0_), channel_id=1, source_target_pairs={{0,1},{1,0},{2,3},{3,2},{4,5},{5,4},{6,7},{7,6},{8,9},{9,8},{10,11... | collective-permute-start | bytes 417800 | tf_op jit(solution)/shard_map/ppermute | solution.py:468
  20.5 4.3 %collective-permute-done.1.refs_1_ = bf16[544,128]{1,0:T(8,128)(2,1)S(1)} collective-permute-done((bf16[544,128]{1,0:T(8,128)(2,1)S(1)}, bf16[544,128]{1,0:T(8,128)(2,1)S(1)}, u32[]{:S(2)}, u32[]{:S(2)}) %collective-permute-start.1) | collective-permute-done | bytes 139296 | tf_op jit(solution)/shard_map/ppermute | solution.py:468
  24.8 1.7 %collective-permute-start.2 = (f32[3,128,128]{2,1,0:T(8,128)S(1)}, f32[3,128,128]{2,1,0:T(8,128)S(1)}, u32[]{:S(2)}, u32[]{:S(2)}) collective-permute-start(f32[3,128,128]{2,1,0:T(8,128)S(1)} %pad_maximum_fusion.4), channel_id=1, source_target_pairs={{0,16},{16,0},{1,17},{17,1},{2,18},{18,2},{3,19},{19,3},{4,20},{20... | collective-permute-start | bytes 589832 | tf_op jit(solution)/shard_map/ppermute | solution.py:550
  26.4 0.7 fusion.18
  27.1 2.6 %collective-permute-start.3 = (bf16[544,128]{1,0:T(8,128)(2,1)S(1)}, bf16[544,128]{1,0:T(8,128)(2,1)S(1)}, u32[]{:S(2)}, u32[]{:S(2)}) collective-permute-start(bf16[544,128]{1,0:T(8,128)(2,1)S(1)} %maximum_maximum_fusion.refs_0_), channel_id=1, source_target_pairs={{0,2},{1,3},{2,0},{3,1},{4,6},{5,7},{6,4},{7,5},{8,10},{9,11},{10,... | collective-permute-start | bytes 417800 | tf_op jit(solution)/shard_map/ppermute | solution.py:468
  29.7 1.3 %collective-permute-start.4 = (bf16[544,128]{1,0:T(8,128)(2,1)S(1)}, bf16[544,128]{1,0:T(8,128)(2,1)S(1)}, u32[]{:S(2)}, u32[]{:S(2)}) collective-permute-start(bf16[544,128]{1,0:T(8,128)(2,1)S(1)} %maximum_maximum_fusion.refs_0_), channel_id=1, source_target_pairs={{0,3},{1,2},{2,1},{3,0},{4,7},{5,6},{6,5},{7,4},{8,11},{9,10},{10,... | collective-permute-start | bytes 417800 | tf_op jit(solution)/shard_map/ppermute | solution.py:468
  31.0 0.3 collective-permute-done.2
  31.4 1.6 %all-to-all-done.query_ref = bf16[4,1040,128]{2,1,0:T(8,128)(2,1)S(1)} async-done(((bf16[4,1040,128]{2,1,0:T(8,128)(2,1)}), bf16[4,1040,128]{2,1,0:T(8,128)(2,1)S(1)}, u32[]{:S(2)}, u32[]{:S(2)}) %all-to-all-start) | async-done | bytes 1064992 | tf_op jit(solution)/shard_map/all_to_all | solution.py:32
  33.2 2.0 %fusion.4 = s32[4,32]{1,0:T(4,128)S(1)} fusion(s32[4,128]{1,0:T(4,128)S(1)} %bitcast.69, s32[]{:T(128)} %bitcast.16, s32[]{:T(128)} %bitcast.15, s32[]{:T(128)} %bitcast.14, s32[]{:T(128)} %axis_index.46, s32[]{:T(128)S(6)} %axis_index.41, s32[4]{0:T(128)S(1)} %slice_reduce_fusion), kind=kLoop, calls=%fused_computation.32 | loop fusion | flops 9088 | bytes 1060 | tf_op jit(solution)/shard_map/jit(_where)/select_n | solution.py:538
  35.2 4.9 %collective-permute-done.3.refs_2_ = bf16[544,128]{1,0:T(8,128)(2,1)S(1)} collective-permute-done((bf16[544,128]{1,0:T(8,128)(2,1)S(1)}, bf16[544,128]{1,0:T(8,128)(2,1)S(1)}, u32[]{:S(2)}, u32[]{:S(2)}) %collective-permute-start.3) | collective-permute-done | bytes 139296 | tf_op jit(solution)/shard_map/ppermute | solution.py:468
  40.1 4.1 %match.1 = f32[2,4,32,128]{3,2,1,0:T(8,128)} custom-call(s32[128]{0:T(128)S(1)} %reshape.42.work_ref, bf16[4,1040,128]{2,1,0:T(8,128)(2,1)S(1)} %all-to-all-done.query_ref, bf16[544,128]{1,0:T(8,128)(2,1)S(1)} %maximum_maximum_fusion.refs_0_, bf16[544,128]{1,0:T(8,128)(2,1)S(1)} %collective-permute-done.1.refs_1_, ...), custom_call_target="tpu_custom_call" | custom-call | flops 1073741824 | bytes 1622016 | tf_op jit(solution)/shard_map/match/pallas_call | solution.py:141
  44.2 1.3 %collective-permute-start.6 = (f32[6,4,128]{2,1,0:T(4,128)S(1)}, f32[6,4,128]{2,1,0:T(4,128)S(1)}, u32[]{:S(2)}, u32[]{:S(2)}) collective-permute-start(f32[6,4,128]{2,1,0:T(4,128)S(1)} %get-tuple-element.22), channel_id=1, source_target_pairs={{0,4},{4,8},{8,12},{1,5},{5,9},{9,13},{2,6},{6,10},{10,14},{3,7},{... | collective-permute-start | bytes 36872 | tf_op jit(solution)/shard_map/ppermute | solution.py:28
  45.5 1.3 %collective-permute-start.5 = (f32[6,4,128]{2,1,0:T(4,128)S(1)}, f32[6,4,128]{2,1,0:T(4,128)S(1)}, u32[]{:S(2)}, u32[]{:S(2)}) collective-permute-start(f32[6,4,128]{2,1,0:T(4,128)S(1)} %get-tuple-element.21), channel_id=1, source_target_pairs={{4,0},{8,4},{12,8},{5,1},{9,5},{13,9},{6,2},{10,6},{14,10},{7,3},{... | collective-permute-start | bytes 36872 | tf_op jit(solution)/shard_map/ppermute | solution.py:28
  46.9 7.3 %all-to-all-start.1 = ((f32[8,32,128]{2,1,0:T(8,128)}), f32[8,32,128]{2,1,0:T(8,128)S(1)}, u32[]{:S(2)}, u32[]{:S(2)}) async-start(f32[8,32,128]{2,1,0:T(8,128)} %bitcast.17), calls=%async_computation.1 | async-start | bytes 262144 | tf_op jit(solution)/shard_map/all_to_all | solution.py:32
  54.3 0.2 slice_bitcast_fusion.1
  54.4 2.7 %collective-permute-start.8 = (f32[6,4,136]{1,2,0:T(8,128)S(1)}, f32[6,4,136]{1,2,0:T(8,128)S(1)}, u32[]{:S(2)}, u32[]{:S(2)}) collective-permute-start(f32[6,4,136]{1,2,0:T(8,128)S(1)} %get-tuple-element.20), channel_id=1, source_target_pairs={{0,1},{1,2},{2,3},{4,5},{5,6},{6,7},{8,9},{9,10},{10,11},{12,13},{... | collective-permute-start | bytes 39176 | tf_op jit(solution)/shard_map/ppermute | solution.py:28
  57.2 1.3 %collective-permute-start.7 = (f32[6,4,136]{1,2,0:T(8,128)S(1)}, f32[6,4,136]{1,2,0:T(8,128)S(1)}, u32[]{:S(2)}, u32[]{:S(2)}) collective-permute-start(f32[6,4,136]{1,2,0:T(8,128)S(1)} %get-tuple-element.19), channel_id=1, source_target_pairs={{1,0},{2,1},{3,2},{5,4},{6,5},{7,6},{9,8},{10,9},{11,10},{13,12},{... | collective-permute-start | bytes 39176 | tf_op jit(solution)/shard_map/ppermute | solution.py:28
  58.5 0.9 %all-to-all-done.1.parts_ref = f32[8,32,128]{2,1,0:T(8,128)S(1)} async-done(((f32[8,32,128]{2,1,0:T(8,128)}), f32[8,32,128]{2,1,0:T(8,128)S(1)}, u32[]{:S(2)}, u32[]{:S(2)}) %all-to-all-start.1) | async-done | bytes 131104 | tf_op jit(solution)/shard_map/all_to_all | solution.py:32
  59.4 0.7 combine.1
  60.1 7.0 %all-to-all-start.2 = ((f32[32,8,128]{2,1,0:T(8,128)}), f32[32,8,128]{2,1,0:T(8,128)S(1)}, u32[]{:S(2)}, u32[]{:S(2)}) async-start(f32[32,8,128]{2,1,0:T(8,128)} %combine.1), calls=%async_computation.2 | async-start | bytes 262144 | tf_op jit(solution)/shard_map/all_to_all | solution.py:32
  67.1 4.8 %collective-permute-done.7 = f32[6,4,136]{1,2,0:T(8,128)S(1)} collective-permute-done((f32[6,4,136]{1,2,0:T(8,128)S(1)}, f32[6,4,136]{1,2,0:T(8,128)S(1)}, u32[]{:S(2)}, u32[]{:S(2)}) %collective-permute-start.7) | collective-permute-done | bytes 13088 | tf_op jit(solution)/shard_map/ppermute | solution.py:28
  72.1 2.7 %spots.1 = (s32[1]{0:T(128)}, s32[16,3,8,128]{3,2,1,0:T(8,128)S(1)}, f32[144,256]{1,0:T(8,128)S(1)}) custom-call(s32[7]{0:T(128)S(1)} %pad_add_fusion.at_ref, f32[2,4,32,128]{3,2,1,0:T(8,128)S(1)} %bitcast.58), custom_call_target="tpu_custom_call" | custom-call | flops 377487360 | bytes 262144 | tf_op jit(solution)/shard_map/spots/pallas_call | solution.py:266
  74.8 2.3 %all-to-all-done.2 = f32[32,8,128]{2,1,0:T(8,128)S(1)} async-done(((f32[32,8,128]{2,1,0:T(8,128)}), f32[32,8,128]{2,1,0:T(8,128)S(1)}, u32[]{:S(2)}, u32[]{:S(2)}) %all-to-all-start.2) | async-done | bytes 131104 | tf_op jit(solution)/shard_map/all_to_all | solution.py:32
  77.1 5.4 %relax.1 = f32[2,128,128]{2,1,0:T(8,128)} custom-call(s32[7]{0:T(128)S(1)} %pad_add_fusion.at_ref, s32[1]{0:T(128)} %get-tuple-element.15.rounds_ref, s32[16,3,8,128]{3,2,1,0:T(8,128)S(1)} %get-tuple-element.16.spot_ref, f32[144,256]{1,0:T(8,128)S(1)} %get-tuple-element.17.count_ref, f32[2,16,8,128]{3,2,1,0:T(8,128)S(1)} %bitcast.57, ...), custom_call_target="tpu_custom_call" | custom-call | tf_op jit(solution)/shard_map/relax/pallas_call | solution.py:559
  (40 shorter events, 1.1 us)
Async XLA Ops:
  1.4 0.9 %copy-start = (bf16[1,1,1,1024,128]{4,3,2,1,0:T(8,128)(2,1)S(1)}, bf16[1,1,1,1024,128]{4,3,2,1,0:T(8,128)(2,1)}, u32[]{:S(2)}) copy-start(bf16[1,1,1,1024,128]{4,3,2,1,0:T(8,128)(2,1)} %param.7) | copy-start | bytes 786436
  2.3 0.7 copy-start.1
  3.0 0.7 copy-start.2
  3.8 9.7 %collective-permute-start = (bf16[1088,128]{1,0:T(8,128)(2,1)S(1)}, bf16[1088,128]{1,0:T(8,128)(2,1)S(1)}, u32[]{:S(2)}, u32[]{:S(2)}) collective-permute-start(bf16[1088,128]{1,0:T(8,128)(2,1)S(1)} %pack.1), channel_id=1, source_target_pairs={{0,16},{16,0},{1,17},{17,1},{2,18},{18,2},{3,19},{19,3},{4,20},{20... | collective-permute-start | bytes 835592 | tf_op jit(solution)/shard_map/ppermute | solution.py:504
  14.7 5.8 %copy-start.3 = (f32[1,2,128,128]{3,2,1,0:T(8,128)S(1)}, f32[1,2,128,128]{3,2,1,0:T(8,128)}, u32[]{:S(2)}) copy-start(f32[1,2,128,128]{3,2,1,0:T(8,128)} %param.12) | copy-start | bytes 393220
  14.7 5.8 %copy-start.4 = (f32[1,128,128]{2,1,0:T(8,128)S(1)}, f32[1,128,128]{2,1,0:T(8,128)}, u32[]{:S(2)}) copy-start(f32[1,128,128]{2,1,0:T(8,128)} %param.13) | copy-start | bytes 196612
  14.7 18.3 %all-to-all-start = ((bf16[4,1040,128]{2,1,0:T(8,128)(2,1)}), bf16[4,1040,128]{2,1,0:T(8,128)(2,1)S(1)}, u32[]{:S(2)}, u32[]{:S(2)}) async-start(bf16[4,1040,128]{2,1,0:T(8,128)(2,1)} %broadcast_in_dim.29), calls=%async_computation | async-start | bytes 2129920 | tf_op jit(solution)/shard_map/all_to_all | solution.py:32
  18.6 6.2 %collective-permute-start.1 = (bf16[544,128]{1,0:T(8,128)(2,1)S(1)}, bf16[544,128]{1,0:T(8,128)(2,1)S(1)}, u32[]{:S(2)}, u32[]{:S(2)}) collective-permute-start(bf16[544,128]{1,0:T(8,128)(2,1)S(1)} %maximum_maximum_fusion.refs_0_), channel_id=1, source_target_pairs={{0,1},{1,0},{2,3},{3,2},{4,5},{5,4},{6,7},{7,6},{8,9},{9,8},{10,11... | collective-permute-start | bytes 417800 | tf_op jit(solution)/shard_map/ppermute | solution.py:468
  24.8 6.6 %collective-permute-start.2 = (f32[3,128,128]{2,1,0:T(8,128)S(1)}, f32[3,128,128]{2,1,0:T(8,128)S(1)}, u32[]{:S(2)}, u32[]{:S(2)}) collective-permute-start(f32[3,128,128]{2,1,0:T(8,128)S(1)} %pad_maximum_fusion.4), channel_id=1, source_target_pairs={{0,16},{16,0},{1,17},{17,1},{2,18},{18,2},{3,19},{19,3},{4,20},{20... | collective-permute-start | bytes 589832 | tf_op jit(solution)/shard_map/ppermute | solution.py:550
  27.1 13.0 %collective-permute-start.3 = (bf16[544,128]{1,0:T(8,128)(2,1)S(1)}, bf16[544,128]{1,0:T(8,128)(2,1)S(1)}, u32[]{:S(2)}, u32[]{:S(2)}) collective-permute-start(bf16[544,128]{1,0:T(8,128)(2,1)S(1)} %maximum_maximum_fusion.refs_0_), channel_id=1, source_target_pairs={{0,2},{1,3},{2,0},{3,1},{4,6},{5,7},{6,4},{7,5},{8,10},{9,11},{10,... | collective-permute-start | bytes 417800 | tf_op jit(solution)/shard_map/ppermute | solution.py:468
  29.7 10.4 %collective-permute-start.4 = (bf16[544,128]{1,0:T(8,128)(2,1)S(1)}, bf16[544,128]{1,0:T(8,128)(2,1)S(1)}, u32[]{:S(2)}, u32[]{:S(2)}) collective-permute-start(bf16[544,128]{1,0:T(8,128)(2,1)S(1)} %maximum_maximum_fusion.refs_0_), channel_id=1, source_target_pairs={{0,3},{1,2},{2,1},{3,0},{4,7},{5,6},{6,5},{7,4},{8,11},{9,10},{10,... | collective-permute-start | bytes 417800 | tf_op jit(solution)/shard_map/ppermute | solution.py:468
  44.2 10.0 %collective-permute-start.6 = (f32[6,4,128]{2,1,0:T(4,128)S(1)}, f32[6,4,128]{2,1,0:T(4,128)S(1)}, u32[]{:S(2)}, u32[]{:S(2)}) collective-permute-start(f32[6,4,128]{2,1,0:T(4,128)S(1)} %get-tuple-element.22), channel_id=1, source_target_pairs={{0,4},{4,8},{8,12},{1,5},{5,9},{9,13},{2,6},{6,10},{10,14},{3,7},{... | collective-permute-start | bytes 36872 | tf_op jit(solution)/shard_map/ppermute | solution.py:28
  45.5 8.7 %collective-permute-start.5 = (f32[6,4,128]{2,1,0:T(4,128)S(1)}, f32[6,4,128]{2,1,0:T(4,128)S(1)}, u32[]{:S(2)}, u32[]{:S(2)}) collective-permute-start(f32[6,4,128]{2,1,0:T(4,128)S(1)} %get-tuple-element.21), channel_id=1, source_target_pairs={{4,0},{8,4},{12,8},{5,1},{9,5},{13,9},{6,2},{10,6},{14,10},{7,3},{... | collective-permute-start | bytes 36872 | tf_op jit(solution)/shard_map/ppermute | solution.py:28
  46.9 12.5 %all-to-all-start.1 = ((f32[8,32,128]{2,1,0:T(8,128)}), f32[8,32,128]{2,1,0:T(8,128)S(1)}, u32[]{:S(2)}, u32[]{:S(2)}) async-start(f32[8,32,128]{2,1,0:T(8,128)} %bitcast.17), calls=%async_computation.1 | async-start | bytes 262144 | tf_op jit(solution)/shard_map/all_to_all | solution.py:32
  54.4 12.6 %collective-permute-start.8 = (f32[6,4,136]{1,2,0:T(8,128)S(1)}, f32[6,4,136]{1,2,0:T(8,128)S(1)}, u32[]{:S(2)}, u32[]{:S(2)}) collective-permute-start(f32[6,4,136]{1,2,0:T(8,128)S(1)} %get-tuple-element.20), channel_id=1, source_target_pairs={{0,1},{1,2},{2,3},{4,5},{5,6},{6,7},{8,9},{9,10},{10,11},{12,13},{... | collective-permute-start | bytes 39176 | tf_op jit(solution)/shard_map/ppermute | solution.py:28
  57.2 14.7 %collective-permute-start.7 = (f32[6,4,136]{1,2,0:T(8,128)S(1)}, f32[6,4,136]{1,2,0:T(8,128)S(1)}, u32[]{:S(2)}, u32[]{:S(2)}) collective-permute-start(f32[6,4,136]{1,2,0:T(8,128)S(1)} %get-tuple-element.19), channel_id=1, source_target_pairs={{1,0},{2,1},{3,2},{5,4},{6,5},{7,6},{9,8},{10,9},{11,10},{13,12},{... | collective-permute-start | bytes 39176 | tf_op jit(solution)/shard_map/ppermute | solution.py:28
  60.1 17.1 %all-to-all-start.2 = ((f32[32,8,128]{2,1,0:T(8,128)}), f32[32,8,128]{2,1,0:T(8,128)S(1)}, u32[]{:S(2)}, u32[]{:S(2)}) async-start(f32[32,8,128]{2,1,0:T(8,128)} %combine.1), calls=%async_computation.2 | async-start | bytes 262144 | tf_op jit(solution)/shard_map/all_to_all | solution.py:32
where the time goes:
time: 83 us; the launch traced here: 82.6 us
  starting transfers between devices  35 us (42%)
  waiting for transfers between devices  25.7 us (31%)
  Pallas kernels  13 us (16%)
  local copies, waits for them, and re-layouts  4.8 us (6%)
  other arithmetic  3.28 us (4%)
  between operations  0.85 us (1%)
    all_to_all x3, starting transfers between devices, exchanged(): return lax.all_to_all(value, axes, split_axis=0, concat_axis=0, tiled=True)  17.9 us
    ppermute x3, waiting for transfers between devices, gathered(): lax.ppermute(value, axis, pairs)  9.15 us
    ppermute x4, starting transfers between devices, passed_along(): return lax.ppermute(value, axis, pairs)  6.58 us
    ppermute x1, waiting for transfers between devices, per_device(): other = lax.ppermute(own, 'sec', swap)  6.57 us
    ppermute x3, starting transfers between devices, gathered(): lax.ppermute(value, axis, pairs)  5.83 us
    pallas_call x1, Pallas kernels, per_device(): pl.pallas_call(functools.partial(relax_kernel, side, halo, extent), out_s...  5.45 us
    ppermute x4, waiting for transfers between devices, passed_along(): return lax.ppermute(value, axis, pairs)  4.85 us
    all_to_all x3, waiting for transfers between devices, exchanged(): return lax.all_to_all(value, axes, split_axis=0, concat_axis=0, tiled=True)  4.8 us
  transfers between devices with their start and end apart: 12, of which 8 were waited for; matrix products, arithmetic and copies ran while one was open for 5% of the time, Pallas kernels for 4%

commit v1 on v0

--- a/solution.py
+++ b/solution.py
@@ -49,21 +49,49 @@
     return pl.BlockSpec(memory_space=pltpu.SMEM)
 
 
-def match_kernel(scale, key_tiles, work_ref, query_ref, *refs):
-    key_refs = refs[:key_tiles]
-    out_ref, key_buf, place_buf, state_buf, list_buf = refs[key_tiles:]
-    shares, tile_rows = out_ref.shape[:2]
+def match_kernel(scale, tile_rows, key_tiles, cand, at_ref, *refs):
+    query_refs, key_refs = refs[:tile_rows], refs[tile_rows : tile_rows + key_tiles]
+    (edge_ref, out_ref, query_buf, key_buf, place_buf, state_buf, found_buf, work_ref, list_buf, sem) = (
+        refs[tile_rows + key_tiles :]
+    )
+    shares = out_ref.shape[0]
     point_total = state_buf.shape[2]
     rows = point_total // LANES // shares
     key_rows = key_buf.shape[1]
     part = key_rows // BLK
     total = key_tiles * part
-    cand = work_ref.shape[0] // tile_rows
+    own_row, share = at_ref[3], at_ref[4]
+
+    for tile, query_ref in enumerate(query_refs):
+        last = query_ref[pl.ds(point_total, PLACE_ROWS), :].astype(jnp.float32).astype(jnp.int32)
+        here = last[0:1] == own_row * shares + share
+        found_buf[pl.ds(tile, 1), :] = jnp.where(here, last[1:2], -1)
+    found = pltpu.make_async_copy(found_buf, work_ref, sem)
+    found.start()
+
+    row_at = lax.broadcasted_iota(jnp.int32, (PLACE_ROWS, LANES), 0)
+    ids = []
+    for tile, key_ref in enumerate(key_refs):
+        col = at_ref[5 + tile_rows + tile]
+        key_buf[col] = key_ref[pl.ds(0, key_rows), :]
+        rest = key_ref[pl.ds(key_rows, key_ref.shape[0] - key_rows), :].astype(jnp.float32)
+        for j in range(part):
+            x, y = rest[j : j + 1, :], rest[part + j : part + j + 1, :]
+            stacked = jnp.where(
+                row_at == 0, x, jnp.where(row_at == 1, y, jnp.where(row_at == 2, 1.0, 0.0))
+            )
+            place_buf[col * part + j] = stacked.astype(jnp.bfloat16)
+        digits = [rest[2 * part + i * rows : 2 * part + (i + 1) * rows] for i in range(DIGITS)]
+        ids.append(sum(digit * float(BASE**i) for i, digit in enumerate(digits)))
+
+    for tile, query_ref in enumerate(query_refs):
+        query_buf[tile] = query_ref[pl.ds(0, point_total), :]
+    found.wait()
 
     number = 0
     for tile in range(tile_rows):
         for i in range(cand):
-            place = work_ref[tile * cand + i]
+            place = work_ref[tile, i]
             list_buf[number] = tile * total + place
             number = number + jnp.where(place >= 0, 1, 0)
         list_buf[number] = -1
@@ -71,20 +99,6 @@
     for i in range(2 * GROUP):
         list_buf[number + i] = -1
     groups = lax.div(number + 2 * GROUP - 1, 2 * GROUP)
-
-    row_at = lax.broadcasted_iota(jnp.int32, (PLACE_ROWS, LANES), 0)
-    ids = []
-    for tile, key_ref in enumerate(key_refs):
-        key_buf[tile] = key_ref[pl.ds(0, key_rows), :]
-        rest = key_ref[pl.ds(key_rows, key_ref.shape[0] - key_rows), :].astype(jnp.float32)
-        for j in range(part):
-            x, y = rest[j : j + 1, :], rest[part + j : part + j + 1, :]
-            stacked = jnp.where(
-                row_at == 0, x, jnp.where(row_at == 1, y, jnp.where(row_at == 2, 1.0, 0.0))
-            )
-            place_buf[tile * part + j] = stacked.astype(jnp.bfloat16)
-        digits = [rest[2 * part + i * rows : 2 * part + (i + 1) * rows] for i in range(DIGITS)]
-        ids.append(sum(digit * float(BASE**i) for i, digit in enumerate(digits)))
 
     state_row = lax.broadcasted_iota(jnp.int32, state_buf.shape[1:], 0)
     for tile in range(tile_rows):
@@ -106,7 +120,7 @@
     def _(group):
         items = [item(group * GROUP + i) for i in range(GROUP)]
         scores = [
-            nt_dot(keys, query_ref[tile, pl.ds(0, point_total), :]) * scale
+            nt_dot(keys, query_buf[tile]) * scale
             for tile, _, keys, _ in items
         ]
         tops = [jnp.max(score, axis=0, keepdims=True) for score in scores]
@@ -123,42 +137,54 @@
             state = state * jnp.exp2(before - both) + added * jnp.exp2(top - both)
             state_buf[tile] = jnp.where(state_row == 3, both, state)
 
+    edge_rows = edge_ref.shape[1]
     for tile in range(tile_rows):
+        to = at_ref[5 + tile]
         for row in range(shares * rows):
             lanes = pl.ds(row * LANES, LANES)
             for place, held in enumerate((3, 2, 0, 1)):
-                out_ref[row // rows, tile, pl.ds(place * rows + row % rows, 1), :] = state_buf[
+                out_ref[row // rows, to, pl.ds(place * rows + row % rows, 1), :] = state_buf[
                     tile, pl.ds(held, 1), lanes
                 ]
         for share in range(shares):
             out_ref[share, tile, pl.ds(4 * rows, key_tiles * rows), :] = jnp.concatenate(ids, axis=0)
-
-
-def match(work, queries, keys, score_factor, shares, point_total, part):
-    tile_rows, key_tiles = queries.shape[0], len(keys)
-    width = queries.shape[2]
+            out_ref[share, tile, pl.ds((4 + key_tiles) * rows, edge_rows), :] = jnp.where(
+                tile > own_row, edge_ref[1], edge_ref[0]
+            )
+
+
+def match(at, queries, keys, edges, score_factor, shares, point_total, part, cand):
+    tile_rows, key_tiles = len(queries), len(keys)
+    width = queries[0].shape[1]
     rows = point_total // LANES // shares
+    total = key_tiles * part
     return pl.pallas_call(
-        functools.partial(match_kernel, score_factor * math.log2(math.e), key_tiles),
+        functools.partial(
+            match_kernel, score_factor * math.log2(math.e), tile_rows, key_tiles, cand
+        ),
         out_shape=jax.ShapeDtypeStruct(
-            (shares, tile_rows, (4 + key_tiles) * rows, LANES), jnp.float32
+            (shares, tile_rows, (4 + key_tiles) * rows + edges.shape[1], LANES), jnp.float32
         ),
-        in_specs=[in_smem()] + in_vmem(1 + key_tiles),
+        in_specs=[in_smem()] + in_vmem(tile_rows + key_tiles + 1),
         out_specs=pl.BlockSpec(memory_space=pltpu.VMEM),
         scratch_shapes=[
+            pltpu.VMEM((tile_rows, point_total, width), jnp.bfloat16),
             pltpu.VMEM((key_tiles, part * BLK, width), jnp.bfloat16),
-            pltpu.VMEM((key_tiles * part, PLACE_ROWS, LANES), jnp.bfloat16),
+            pltpu.VMEM((total, PLACE_ROWS, LANES), jnp.bfloat16),
             pltpu.VMEM((tile_rows, 8, point_total), jnp.float32),
-            pltpu.SMEM((work.shape[0] + 2 * GROUP + tile_rows,), jnp.int32),
+            pltpu.VMEM((tile_rows, LANES), jnp.int32),
+            pltpu.SMEM((tile_rows, LANES), jnp.int32),
+            pltpu.SMEM((tile_rows * (cand + 1) + 2 * GROUP + 1,), jnp.int32),
+            pltpu.SemaphoreType.DMA,
         ],
         compiler_params=pltpu.CompilerParams(vmem_limit_bytes=VMEM_BYTES),
         cost_estimate=pl.CostEstimate(
-            flops=tile_rows * key_tiles * part * point_total * BLK * width,
-            bytes_accessed=2 * (queries.size + key_tiles * keys[0].size),
-            transcendentals=tile_rows * key_tiles * part * point_total * BLK // 4,
+            flops=tile_rows * total * point_total * BLK * width,
+            bytes_accessed=2 * (tile_rows * queries[0].size + key_tiles * keys[0].size),
+            transcendentals=tile_rows * total * point_total * BLK // 4,
         ),
         name="match",
-    )(work, queries, *keys)
+    )(at, *queries, *keys, edges)
 
 
 def combine_kernel(parts_ref, place_ref, out_ref):
@@ -249,7 +275,7 @@
         tile_of = row = col = jnp.full(number.shape, -1, jnp.int32)
         for at, (i, j) in enumerate(tiles):
             here = hit_buf[0, at] == k
-            tile_of = jnp.where(here, i * key_tiles + at_ref[3 + j], tile_of)
+            tile_of = jnp.where(here, i * key_tiles + at_ref[5 + tile_rows + j], tile_of)
             row = jnp.where(here, hit_buf[1, at], row)
             col = jnp.where(here, hit_buf[2, at], col)
         spot_ref[k, 0] = tile_of
@@ -375,15 +401,10 @@
         out_ref[c] = moving[0][c][0][0:side, 0:side]
 
 
-def with_halo(value, halo, wide):
-    side = value.shape[1]
-    after = passed_along(value[:, :halo], "ty", -1)
-    before = passed_along(value[:, side - halo :], "ty", 1)
-    value = jnp.concatenate([value, after, before], axis=1)
-    after = passed_along(value[:, :, :halo].swapaxes(1, 2), "tx", -1).swapaxes(1, 2)
-    before = passed_along(value[:, :, side - halo :].swapaxes(1, 2), "tx", 1).swapaxes(1, 2)
-    gap = jnp.zeros(value.shape[:2] + (wide - side - 2 * halo,), value.dtype)
-    return jnp.concatenate([value, after, gap, before], axis=2)
+def col_edges(value, halo):
+    after = passed_along(value[:, :, :halo].swapaxes(1, 2), "tx", -1)
+    before = passed_along(value[:, :, value.shape[2] - halo :].swapaxes(1, 2), "tx", 1)
+    return jnp.concatenate([after, before], axis=1)
 
 
 def sweeps(moving, gains, sums, number, at, side, halo, extent):
@@ -419,53 +440,111 @@
     return moving[:, :side, :side]
 
 
-def pack_kernel(desc_hbm, place_ref, ids_ref, list_ref, out_ref, sem):
-    points = desc_hbm.shape[0]
-    copy = pltpu.make_async_copy(desc_hbm, out_ref.at[pl.ds(0, points), :], sem)
-    copy.start()
-
-    def digit(value, i):
-        return ((value >> (i * BASE.bit_length() - i)) & (BASE - 1)).astype(jnp.float32)
+def pack_kernel(
+    shares,
+    tile_cols,
+    desc_hbm,
+    place_hbm,
+    ids_hbm,
+    list_hbm,
+    count_hbm,
+    first_ref,
+    second_ref,
+    place_ref,
+    ids_ref,
+    list_ref,
+    count_ref,
+    sems,
+):
+    half = second_ref.shape[0]
+    copies = [
+        pltpu.make_async_copy(source, target, sems.at[i])
+        for i, (source, target) in enumerate(
+            (
+                (place_hbm, place_ref),
+                (ids_hbm, ids_ref),
+                (list_hbm, list_ref),
+                (count_hbm, count_ref),
+                (desc_hbm.at[pl.ds(0, half), :], first_ref.at[pl.ds(0, half), :]),
+                (desc_hbm.at[pl.ds(half, half), :], second_ref),
+            )
+        )
+    ]
+    for copy in copies:
+        copy.start()
+    for copy in copies[:4]:
+        copy.wait()
 
     def cut(row):
         return [row[:, i : i + LANES] for i in range(0, row.shape[1], LANES)]
 
-    place, ids, listed = place_ref[...].astype(jnp.float32), ids_ref[...], list_ref[...]
+    place, ids, blocks = place_ref[...].astype(jnp.float32), ids_ref[...], list_ref[...]
     rows = cut(place[0:1]) + cut(place[1:2])
     for i in range(DIGITS):
-        rows += cut(digit(ids, i))
-    last = [digit(listed, 0), digit(listed, 1)]
-    count = out_ref.shape[0] - points
+        digit = lax.rem(lax.div(ids, BASE**i), BASE)
+        rows += cut(digit.astype(jnp.float32))
+    per_tile = place.shape[1] // BLK
+    part = per_tile // shares
+    tile, within = lax.div(blocks, per_tile), lax.rem(blocks, per_tile)
+    device = lax.div(tile, tile_cols) * shares + lax.div(within, part)
+    spot = lax.rem(tile, tile_cols) * part + lax.rem(within, part)
+    live = lax.broadcasted_iota(jnp.int32, blocks.shape, 1) < count_ref[0, 0]
+    device = jnp.where(live, device, BASE - 1)
+    count = first_ref.shape[0] - half
     gap = jnp.zeros((count - len(rows) - PLACE_ROWS, LANES), jnp.float32)
-    end = jnp.zeros((PLACE_ROWS - len(last), LANES), jnp.float32)
-    rows += ([gap] if gap.shape[0] else []) + last + [end]
-    out_ref[pl.ds(points, count), :] = jnp.concatenate(rows, axis=0).astype(jnp.bfloat16)
-    copy.wait()
-
-
-def pack(desc, place, ids, listed):
-    per_tile = ids.shape[1] // LANES
-    rows = -(-(2 + DIGITS) * per_tile // 16) * 16 + PLACE_ROWS
+    end = jnp.zeros((PLACE_ROWS - 2, LANES), jnp.float32)
+    rows += ([gap] if gap.shape[0] else []) + [v.astype(jnp.float32) for v in (device, spot)] + [end]
+    first_ref[pl.ds(half, count), :] = jnp.concatenate(rows, axis=0).astype(jnp.bfloat16)
+    for copy in copies[4:]:
+        copy.wait()
+
+
+def pack(desc, place, ids, blocks, count, shares, tile_cols):
+    points, width = desc.shape
+    half = points // 2
+    rows = -(-(2 + DIGITS) * (points // LANES) // 16) * 16 + PLACE_ROWS
     return pl.pallas_call(
-        pack_kernel,
-        out_shape=jax.ShapeDtypeStruct((desc.shape[0] + rows, LANES), jnp.bfloat16),
-        in_specs=[pl.BlockSpec(memory_space=pl.ANY)] + in_vmem(3),
-        out_specs=pl.BlockSpec(memory_space=pltpu.VMEM),
-        scratch_shapes=[pltpu.SemaphoreType.DMA],
+        functools.partial(pack_kernel, shares, tile_cols),
+        out_shape=(
+            jax.ShapeDtypeStruct((half + rows, width), jnp.bfloat16),
+            jax.ShapeDtypeStruct((half, width), jnp.bfloat16),
+        ),
+        in_specs=[pl.BlockSpec(memory_space=pl.ANY)] * 5,
+        out_specs=(pl.BlockSpec(memory_space=pltpu.VMEM),) * 2,
+        scratch_shapes=[
+            pltpu.VMEM(place.shape, place.dtype),
+            pltpu.VMEM(ids.shape, ids.dtype),
+            pltpu.VMEM(blocks.shape, blocks.dtype),
+            pltpu.SMEM(count.shape, count.dtype),
+            pltpu.SemaphoreType.DMA((6,)),
+        ],
         compiler_params=pltpu.CompilerParams(vmem_limit_bytes=VMEM_BYTES),
         name="pack",
-    )(desc, place, ids, listed)
-
-
-def gathered(value, axis):
+    )(desc, place, ids, blocks, count)
+
+
+def turns(axis):
     devices, here = lax.axis_size(axis), lax.axis_index(axis)
     if devices & (devices - 1):
-        partners = [[(i, (i + j) % devices) for i in range(devices)] for j in range(1, devices)]
-        place = jnp.mod(here - jnp.arange(devices), devices)
-    else:
-        partners = [[(i, i ^ j) for i in range(devices)] for j in range(1, devices)]
-        place = here ^ jnp.arange(devices)
-    return [value] + [lax.ppermute(value, axis, pairs) for pairs in partners], place
+        pairs = [[(i, (i + j) % devices) for i in range(devices)] for j in range(1, devices)]
+        return pairs, jnp.mod(here - jnp.arange(devices), devices)
+    pairs = [[(i, i ^ j) for i in range(devices)] for j in range(1, devices)]
+    return pairs, here ^ jnp.arange(devices)
+
+
+def gathered(value, axis):
+    return [value] + [lax.ppermute(value, axis, pairs) for pairs in turns(axis)[0]]
+
+
+def handed_on(value, axis):
+    devices = lax.axis_size(axis)
+    if devices & (devices - 1):
+        return gathered(value, axis)
+    held = {0: value}
+    for at in sorted(range(1, devices), key=lambda at: (at.bit_count(), -at)):
+        by = at & -at
+        held[at] = lax.ppermute(held[at ^ by], axis, [(i, i ^ by) for i in range(devices)])
+    return [held[i] for i in range(devices)]
 
 
 def per_device(
@@ -486,10 +565,16 @@
     part = per_tile // shares
     key_rows = part * BLK
 
-    listed = jnp.concatenate([candidate_blocks[0, 0, 0], candidate_count[0, 0, 0][None]])
-    listed = jnp.pad(listed, (0, LANES - cand - 1))[None]
-    own = pack(descriptors[0, 0, 0], positions[0, 0, 0], vertex_ids[0, 0], listed)
-    own_mesh = jnp.concatenate([displacement[0], stiffness], axis=0)
+    first_half, second_half = pack(
+        descriptors[0, 0, 0],
+        positions[0, 0, 0],
+        vertex_ids[0, 0],
+        jnp.pad(candidate_blocks[0, 0], ((0, 0), (0, LANES - cand))),
+        candidate_count[0, 0][None],
+        shares,
+        tile_cols,
+    )
+    half = point_total // 2
     swap = [(i, 1 - i) for i in range(2)]
 
     def of_share(rows):
@@ -498,63 +583,85 @@
             rows = jnp.where(sec_index == 0, rows[:, 0], rows[:, 1])
         return rows.reshape(-1, LANES)
 
+    place_rows = slice(half, half + 2 * per_tile)
+    id_rows = slice(half + 2 * per_tile, half + (2 + DIGITS) * per_tile)
     if shares == 2:
         first = sec_index == 0
         share = sec_index
-        other = lax.ppermute(own, "sec", swap)
-        query = jnp.where(first, own, other)
-        key = jnp.where(first, other[:key_rows], own[key_rows:point_total])
-        key_place = jnp.where(
-            first,
-            other[point_total : point_total + 2 * per_tile],
-            own[point_total : point_total + 2 * per_tile],
-        )
+        other = lax.ppermute(first_half, "sec", swap)
+        came = passed_along(second_half, "sec", 1)
+        query = jnp.where(first, first_half, other)
+        key = jnp.where(first, other[:half], second_half)
+        key_place = jnp.where(first, other[place_rows], first_half[place_rows])
+        rest = jnp.where(first, second_half, came)
     else:
         share = 0
-        query = passed_along(own, "sec", 1)
-        key, key_place = own[:point_total], own[point_total : point_total + 2 * per_tile]
-    rest = query[point_total:]
-    place = of_share(rest[: 2 * per_tile])
-    ids = of_share(rest[2 * per_tile : (2 + DIGITS) * per_tile])
+        query, rest = (passed_along(v, "sec", 1) for v in (first_half, second_half))
+        key = jnp.concatenate([first_half[:half], second_half], axis=0)
+        key_place = first_half[place_rows]
+    place, ids = of_share(query[place_rows]), of_share(query[id_rows])
     filler = jnp.zeros((-(2 + DIGITS) * part % 16, LANES), jnp.bfloat16)
     key = jnp.concatenate([key, of_share(key_place), ids, filler], axis=0)
-    query = jnp.concatenate([query[:point_total], rest[-PLACE_ROWS:]], axis=0)
-
-    keys, key_col = gathered(key, "tx")
-    queries = spread(query, "ty")
-
-    lists = queries[:, point_total : point_total + 2].astype(jnp.int32)
-    lists = lists[:, 0] + BASE * lists[:, 1]
-    blocks, counts = lists[:, :cand], lists[:, cand : cand + 1]
-    tile_of, within = blocks // per_tile, blocks % per_tile
-    slot_of = jnp.zeros_like(tile_of)
-    for i in range(tile_cols):
-        slot_of = jnp.where(tile_of % tile_cols == key_col[i], i, slot_of)
-    here = (
-        (jnp.arange(cand)[None, :] < counts)
-        & (tile_of // tile_cols == lax.axis_index("ty"))
-        & (within // part == share)
-    )
-    work = jnp.where(here, slot_of * part + within % part, -1).reshape(-1).astype(jnp.int32)
+    query = jnp.concatenate([query[:half], rest, query[-PLACE_ROWS:]], axis=0)
+    keys = gathered(key, "tx")
+    queries = handed_on(query, "ty")
     at = jnp.concatenate(
         [
             jnp.stack([lax.axis_index("ty") * side, lax.axis_index("tx") * side, sec_index]),
-            key_col,
+            jnp.stack([lax.axis_index("ty"), jnp.asarray(share)]),
+            turns("ty")[1],
+            turns("tx")[1],
         ]
     ).astype(jnp.int32)
     extent = (side * tile_rows, side * tile_cols)
     sum_shape = pltpu.VMEM((2, -(-span // 16) * 16, wide), jnp.float32)
 
+    own_mesh = jnp.concatenate([displacement[0], stiffness], axis=0)
+    cols = col_edges(own_mesh, halo)
+    top, end = own_mesh[:, :halo], own_mesh[:, side - halo :]
+    corners = [
+        jnp.pad(v.swapaxes(1, 2), ((0, 0), (0, 0), (0, side - 2 * halo)))
+        for v in (cols[:, :, :halo], cols[:, :, side - halo :])
+    ]
+    edges = jnp.stack([jnp.concatenate(v, axis=0) for v in ((top, corners[0]), (end, corners[1]))])
+    edges = edges.reshape(2, -1, LANES)
+    meshes = [jnp.concatenate([own_mesh, cols], axis=1)]
     if shares == 2:
-        tied, keys[1] = lax.optimization_barrier((own_mesh, keys[1]))
-        own_mesh = jnp.concatenate([own_mesh, lax.ppermute(tied, "sec", swap)], axis=0)
-    parts = match(work, queries, keys, 16.0 / width, shares, point_total, part)
-    own_mesh, parts = lax.optimization_barrier((own_mesh, parts))
-    mesh_values = with_halo(own_mesh, halo, wide)
+        tied, queries[1] = lax.optimization_barrier((meshes[0], queries[1]))
+        meshes.append(lax.ppermute(tied, "sec", swap))
+    parts = match(at, queries, keys, edges, 16.0 / width, shares, point_total, part, cand)
+    shape = parts.shape
+    parts = exchanged(parts.reshape((-1,) + shape[2:]), ("sec", "ty") if shares == 2 else "ty")
+    pulls = combine(parts, place, shares * tiles)
+    parts, pulls = lax.optimization_barrier((parts, pulls))
+
+    def edge_rows(by):
+        near = lax.axis_index("ty") + by
+        rows = parts.reshape(shape)[:, :, -edges.shape[1] :]
+        rows = lax.dynamic_index_in_dim(rows, jnp.clip(near, 0, tile_rows - 1), 1, keepdims=False)
+        rows = jnp.where((near >= 0) & (near < tile_rows), rows, 0.0)
+        rows = rows.reshape(shares, 2, 3, halo, side)
+        if shares == 2:
+            rows = jnp.where(first, rows, rows[::-1])
+        rows = rows.reshape(-1, 3, halo, side)
+        return [
+            jnp.concatenate([rows[2 * i], rows[2 * i + 1, :, :, : 2 * halo]], axis=2)
+            for i in range(shares)
+        ]
+
+    after, before = edge_rows(1), edge_rows(-1)
+    framed = []
+    for i, mesh in enumerate(meshes):
+        sides = mesh[:, side:].swapaxes(1, 2)
+        whole = jnp.concatenate([mesh[:, :side], sides], axis=2)
+        framed.append(jnp.concatenate([whole, after[i], before[i]], axis=1))
+    framed = jnp.concatenate(framed, axis=0)
+    gap = jnp.zeros(framed.shape[:2] + (wide - span,), framed.dtype)
+    mesh_values = jnp.concatenate(
+        [framed[:, :, : side + halo], gap, framed[:, :, side + halo :]], axis=2
+    )
     if shares == 2:
-        shape = parts.shape
-        parts = exchanged(parts.reshape((-1,) + shape[2:]), ("sec", "ty"))
-        points = exchanged(combine(parts, place, 2 * tiles), ("sec", "ty", "tx"))
+        points = exchanged(pulls, ("sec", "ty", "tx"))
         rounds, spot, number = spots(side, halo, tile_cols, wide, at, parts.reshape(shape), part)
         relaxed = pl.pallas_call(
             functools.partial(relax_kernel, side, halo, extent),
@@ -567,8 +674,7 @@
         )(at, rounds, spot, number, points.reshape(2, tiles, -1, LANES), mesh_values)
         return relaxed[None]
 
-    parts = exchanged(parts[0], "ty")
-    points = passed_along(exchanged(combine(parts, place, tiles), ("ty", "tx")), "sec", -1)
+    points = passed_along(exchanged(pulls, ("ty", "tx")), "sec", -1)
     parts = passed_along(parts, "sec", -1)
     rounds, spot, number = spots(side, halo, tile_cols, wide, at, parts[None], part)
     sums = pl.pallas_call(

time: 83 us -> 80.2 us (0.966)
  starting transfers between devices: 35 us -> 25.2 us
  waiting for transfers between devices: 25.7 us -> 32 us
  Pallas kernels: 13 us -> 15.9 us
  other arithmetic: 3.28 us -> 1.01 us
    ppermute x2 -> x5, waiting for transfers between devices: 6.89 us -> 18 us  [the longest x1 10.9 us: per_device(): meshes.append(lax.ppermute(tied, 'sec', swap))]
    all_to_all x3 -> x2, starting transfers between devices: 17.9 us -> 7.24 us  [exchanged(): return lax.all_to_all(value, axes, split_axis=0, concat_axis=0, tiled=True)]
    ppermute x3, waiting for transfers between devices: 9.15 us -> 0.01 us  [gathered(): lax.ppermute(value, axis, pairs)]
    all_to_all x3 -> x2, waiting for transfers between devices: 4.8 us -> 10.9 us  [exchanged(): return lax.all_to_all(value, axes, split_axis=0, concat_axis=0, tiled=True)]
    pallas_call x1, Pallas kernels: 4.09 us -> 6.43 us  [match(): pl.pallas_call(functools.partial(match_kernel, score_factor * math.log2(m...]
    select_n x4 -> x6, other arithmetic: 2.01 us -> 0.08 us  [the longest x1 0.02 us: per_device(): key = jnp.where(first, other[:half], second_half)]
    ppermute x4 -> x3, waiting for transfers between devices: 4.85 us -> 3.11 us  [passed_along(): return lax.ppermute(value, axis, pairs)]
    ppermute x4 -> x3, starting transfers between devices: 6.58 us -> 7.85 us  [passed_along(): return lax.ppermute(value, axis, pairs)]
  transfers between devices with their start and end apart: 12 -> 13, of which waited for: 8 -> 6; matrix products, arithmetic and copies ran while one was open for 5% -> 2% of each run, Pallas kernels for 4% -> 3%
where the time goes in v1:
time: 80.2 us; the launch traced here: 79.8 us
  waiting for transfers between devices  32 us (40%)
  starting transfers between devices  25.2 us (31%)
  Pallas kernels  15.9 us (20%)
  local copies, waits for them, and re-layouts  4.57 us (6%)
  between operations  1.03 us (1%)
  other arithmetic  1.01 us (1%)
    ppermute x1, waiting for transfers between devices, per_device(): meshes.append(lax.ppermute(tied, 'sec', swap))  10.9 us
    all_to_all x2, waiting for transfers between devices, exchanged(): return lax.all_to_all(value, axes, split_axis=0, concat_axis=0, tiled=True)  10.9 us
    ppermute x3, starting transfers between devices, passed_along(): return lax.ppermute(value, axis, pairs)  7.85 us
    all_to_all x2, starting transfers between devices, exchanged(): return lax.all_to_all(value, axes, split_axis=0, concat_axis=0, tiled=True)  7.24 us
    ppermute x3, waiting for transfers between devices, handed_on(): lax.ppermute(held[at ^ by], axis, [(i, i ^ by) for i in range(devices)])  7.02 us
    pallas_call x1, Pallas kernels, match(): pl.pallas_call(functools.partial(match_kernel, score_factor * math.log2(m...  6.43 us
    pallas_call x1, Pallas kernels, per_device(): pl.pallas_call(functools.partial(relax_kernel, side, halo, extent), out_s...  5.45 us
    ppermute x3, starting transfers between devices, gathered(): lax.ppermute(value, axis, pairs)  5.3 us
  transfers between devices with their start and end apart: 13, of which 6 were waited for; matrix products, arithmetic and copies ran while one was open for 2% of the time, Pallas kernels for 3%

profile of v1, /device:TPU:0, one launch (start us, length us, event | category | flops | bytes accessed | tf_op | source)
XLA Modules:
  0.0 79.8 jit_solution(4289587233585943508)
XLA Ops:
  0.7 0.6 copy-done.6
  1.3 0.7 copy-done.2
  2.0 0.9 %copy-done = bf16[1,1,1,1024,128]{4,3,2,1,0:T(8,128)(2,1)S(1)} copy-done((bf16[1,1,1,1024,128]{4,3,2,1,0:T(8,128)(2,1)S(1)}, bf16[1,1,1,1024,128]{4,3,2,1,0:T(8,128)(2,1)}, u32[]{:S(2)}) %copy-start) | copy-done | bytes 262168
  3.0 0.6 pack.1
  3.6 3.0 %collective-permute-start = (bf16[576,128]{1,0:T(8,128)(2,1)S(1)}, bf16[576,128]{1,0:T(8,128)(2,1)S(1)}, u32[]{:S(2)}, u32[]{:S(2)}) collective-permute-start(bf16[576,128]{1,0:T(8,128)(2,1)S(1)} %get-tuple-element.14), channel_id=1, source_target_pairs={{0,16},{16,0},{1,17},{17,1},{2,18},{18,2},{3,19},{19,3},{4,20},{20... | collective-permute-start | bytes 442376 | tf_op jit(solution)/shard_map/ppermute | solution.py:591
  6.6 1.9 %collective-permute-start.1 = (bf16[512,128]{1,0:T(8,128)(2,1)S(1)}, bf16[512,128]{1,0:T(8,128)(2,1)S(1)}, u32[]{:S(2)}, u32[]{:S(2)}) collective-permute-start(bf16[512,128]{1,0:T(8,128)(2,1)S(1)} %get-tuple-element.15), channel_id=1, source_target_pairs={{0,16},{1,17},{2,18},{3,19},{4,20},{5,21},{6,22},{7,23},{8,24},{9,... | collective-permute-start | bytes 393224 | tf_op jit(solution)/shard_map/ppermute | solution.py:28
  8.7 1.3 %collective-permute-start.2 = (f32[3,4,128]{1,2,0:T(8,128)S(1)}, f32[3,4,128]{1,2,0:T(8,128)S(1)}, u32[]{:S(2)}, u32[]{:S(2)}) collective-permute-start(f32[3,4,128]{1,2,0:T(8,128)S(1)} %get-tuple-element.27), channel_id=1, source_target_pairs={{1,0},{2,1},{3,2},{5,4},{6,5},{7,6},{9,8},{10,9},{11,10},{13,12},{... | collective-permute-start | bytes 18440 | tf_op jit(solution)/shard_map/ppermute | solution.py:28
  10.0 4.6 %collective-permute-start.3 = (f32[3,4,128]{1,2,0:T(8,128)S(1)}, f32[3,4,128]{1,2,0:T(8,128)S(1)}, u32[]{:S(2)}, u32[]{:S(2)}) collective-permute-start(f32[3,4,128]{1,2,0:T(8,128)S(1)} %get-tuple-element.28), channel_id=1, source_target_pairs={{0,1},{1,2},{2,3},{4,5},{5,6},{6,7},{8,9},{9,10},{10,11},{12,13},{... | collective-permute-start | bytes 18440 | tf_op jit(solution)/shard_map/ppermute | solution.py:28
  14.7 0.1 copy.29
  15.1 1.9 %collective-permute-done.2 = f32[3,4,128]{1,2,0:T(8,128)S(1)} collective-permute-done((f32[3,4,128]{1,2,0:T(8,128)S(1)}, f32[3,4,128]{1,2,0:T(8,128)S(1)}, u32[]{:S(2)}, u32[]{:S(2)}) %collective-permute-start.2) | collective-permute-done | bytes 6176 | tf_op jit(solution)/shard_map/ppermute | solution.py:28
  17.0 1.2 %collective-permute-done.3 = f32[3,4,128]{1,2,0:T(8,128)S(1)} collective-permute-done((f32[3,4,128]{1,2,0:T(8,128)S(1)}, f32[3,4,128]{1,2,0:T(8,128)S(1)}, u32[]{:S(2)}, u32[]{:S(2)}) %collective-permute-start.3) | collective-permute-done | bytes 6176 | tf_op jit(solution)/shard_map/ppermute | solution.py:28
  18.3 0.1 maximum_bitcast_fusion
  18.4 0.1 pad_maximum_fusion.2
  18.6 0.6 copy-done.5
  19.3 0.9 %slice-done.1 = bf16[512,128]{1,0:T(8,128)(2,1)S(1)} async-done(((bf16[576,128]{1,0:T(8,128)(2,1)}), bf16[512,128]{1,0:T(8,128)(2,1)S(1)}, s32[]{:S(2)}) %slice-start.1) | async-done | bytes 131096 | tf_op jit(solution)/shard_map/slice | solution.py:605
  20.2 1.7 %collective-permute-start.5 = (bf16[1040,128]{1,0:T(8,128)(2,1)S(1)}, bf16[1040,128]{1,0:T(8,128)(2,1)S(1)}, u32[]{:S(2)}, u32[]{:S(2)}) collective-permute-start(bf16[1040,128]{1,0:T(8,128)(2,1)S(1)} %pad_maximum_fusion.3.refs_0_), channel_id=1, source_target_pairs={{0,8},{4,12},{8,0},{12,4},{1,9},{5,13},{9,1},{13,5},{2,10},{6,14},... | collective-permute-start | bytes 798728 | tf_op jit(solution)/shard_map/ppermute | solution.py:546
  22.0 7.0 %collective-permute-done.5.refs_2_ = bf16[1040,128]{1,0:T(8,128)(2,1)S(1)} collective-permute-done((bf16[1040,128]{1,0:T(8,128)(2,1)S(1)}, bf16[1040,128]{1,0:T(8,128)(2,1)S(1)}, u32[]{:S(2)}, u32[]{:S(2)}) %collective-permute-start.5) | collective-permute-done | bytes 266272 | tf_op jit(solution)/shard_map/ppermute | solution.py:546
  29.1 0.1 maximum_maximum_fusion.1.refs_4_
  29.2 2.5 %collective-permute-start.7 = (bf16[544,128]{1,0:T(8,128)(2,1)S(1)}, bf16[544,128]{1,0:T(8,128)(2,1)S(1)}, u32[]{:S(2)}, u32[]{:S(2)}) collective-permute-start(bf16[544,128]{1,0:T(8,128)(2,1)S(1)} %maximum_maximum_fusion.1.refs_4_), channel_id=1, source_target_pairs={{0,1},{1,0},{2,3},{3,2},{4,5},{5,4},{6,7},{7,6},{8,9},{9,8},{10,11... | collective-permute-start | bytes 417800 | tf_op jit(solution)/shard_map/ppermute | solution.py:536
  31.7 2.8 %collective-permute-start.8 = (bf16[544,128]{1,0:T(8,128)(2,1)S(1)}, bf16[544,128]{1,0:T(8,128)(2,1)S(1)}, u32[]{:S(2)}, u32[]{:S(2)}) collective-permute-start(bf16[544,128]{1,0:T(8,128)(2,1)S(1)} %maximum_maximum_fusion.1.refs_4_), channel_id=1, source_target_pairs={{0,2},{1,3},{2,0},{3,1},{4,6},{5,7},{6,4},{7,5},{8,10},{9,11},{10,... | collective-permute-start | bytes 417800 | tf_op jit(solution)/shard_map/ppermute | solution.py:536
  34.5 10.9 %collective-permute-done.10 = f32[3,136,128]{1,2,0:T(8,128)S(1)} collective-permute-done((f32[3,136,128]{1,2,0:T(8,128)S(1)}, f32[3,136,128]{1,2,0:T(8,128)S(1)}, u32[]{:S(2)}, u32[]{:S(2)}) %collective-permute-start.10) | collective-permute-done | bytes 208928 | tf_op jit(solution)/shard_map/ppermute | solution.py:631
  45.5 0.1 copy.36
  45.7 6.4 %match.1 = f32[2,4,56,128]{3,2,1,0:T(8,128)} custom-call(s32[13]{0:T(128)S(1)} %concatenate.56.at_ref, bf16[1040,128]{1,0:T(8,128)(2,1)S(1)} %pad_maximum_fusion.3.refs_0_, bf16[1040,128]{1,0:T(8,128)(2,1)S(1)} %collective-permute-done.4.refs_1_, bf16[1040,128]{1,0:T(8,128)(2,1)S(1)} %collective-permute-done.5.refs_2_, ...), custom_call_target="tpu_custom_call" | custom-call | flops 1073741824 | bytes 1622016 | tf_op jit(solution)/shard_map/match/pallas_call | solution.py:161
  52.1 3.4 %all-to-all-start = ((f32[8,56,128]{2,1,0:T(8,128)}), f32[8,56,128]{2,1,0:T(8,128)S(1)}, u32[]{:S(2)}, u32[]{:S(2)}) async-start(f32[8,56,128]{2,1,0:T(8,128)} %bitcast.19), calls=%async_computation | async-start | bytes 458752 | tf_op jit(solution)/shard_map/all_to_all | solution.py:32
  55.5 5.7 %all-to-all-done.parts_ref = f32[8,56,128]{2,1,0:T(8,128)S(1)} async-done(((f32[8,56,128]{2,1,0:T(8,128)}), f32[8,56,128]{2,1,0:T(8,128)S(1)}, u32[]{:S(2)}, u32[]{:S(2)}) %all-to-all-start) | async-done | bytes 229408 | tf_op jit(solution)/shard_map/all_to_all | solution.py:32
  61.3 0.7 combine.1
  62.1 3.8 %all-to-all-start.1 = ((f32[32,8,128]{2,1,0:T(8,128)}), f32[32,8,128]{2,1,0:T(8,128)S(1)}, u32[]{:S(2)}, u32[]{:S(2)}) async-start(f32[32,8,128]{2,1,0:T(8,128)} %combine.1), calls=%async_computation.1 | async-start | bytes 262144 | tf_op jit(solution)/shard_map/all_to_all | solution.py:32
  66.0 2.7 %spots.1 = (s32[1]{0:T(128)}, s32[16,3,8,128]{3,2,1,0:T(8,128)S(1)}, f32[144,256]{1,0:T(8,128)S(1)}) custom-call(s32[13]{0:T(128)S(1)} %concatenate.56.at_ref, f32[2,4,56,128]{3,2,1,0:T(8,128)S(1)} %bitcast.82), custom_call_target="tpu_custom_call" | custom-call | flops 377487360 | bytes 458752 | tf_op jit(solution)/shard_map/spots/pallas_call | solution.py:292
  68.8 0.2 slice.165
  68.9 0.2 pad_maximum_fusion.mesh_ref
  69.1 5.2 %all-to-all-done.1 = f32[32,8,128]{2,1,0:T(8,128)S(1)} async-done(((f32[32,8,128]{2,1,0:T(8,128)}), f32[32,8,128]{2,1,0:T(8,128)S(1)}, u32[]{:S(2)}, u32[]{:S(2)}) %all-to-all-start.1) | async-done | bytes 131104 | tf_op jit(solution)/shard_map/all_to_all | solution.py:32
  74.3 5.4 %relax.1 = f32[2,128,128]{2,1,0:T(8,128)} custom-call(s32[13]{0:T(128)S(1)} %concatenate.56.at_ref, s32[1]{0:T(128)} %get-tuple-element.18.rounds_ref, s32[16,3,8,128]{3,2,1,0:T(8,128)S(1)} %get-tuple-element.19.spot_ref, f32[144,256]{1,0:T(8,128)S(1)} %get-tuple-element.20.count_ref, f32[2,16,8,128]{3,2,1,0:T(8,128)S(1)} %bitcast.83, ...), custom_call_target="tpu_custom_call" | custom-call | tf_op jit(solution)/shard_map/relax/pallas_call | solution.py:666
  (57 shorter events, 0.9 us)
Async XLA Ops:
  0.7 0.7 copy-start.6
  1.3 0.7 copy-start.2
  1.3 0.7 copy-start.1
  2.0 0.9 %copy-start = (bf16[1,1,1,1024,128]{4,3,2,1,0:T(8,128)(2,1)S(1)}, bf16[1,1,1,1024,128]{4,3,2,1,0:T(8,128)(2,1)}, u32[]{:S(2)}) copy-start(bf16[1,1,1,1024,128]{4,3,2,1,0:T(8,128)(2,1)} %param.7) | copy-start | bytes 786436
  3.0 5.6 %copy-start.3 = (f32[1,2,128,128]{3,2,1,0:T(8,128)S(1)}, f32[1,2,128,128]{3,2,1,0:T(8,128)}, u32[]{:S(2)}) copy-start(f32[1,2,128,128]{3,2,1,0:T(8,128)} %param.12) | copy-start | bytes 393220
  3.0 5.6 %copy-start.4 = (f32[1,128,128]{2,1,0:T(8,128)S(1)}, f32[1,128,128]{2,1,0:T(8,128)}, u32[]{:S(2)}) copy-start(f32[1,128,128]{2,1,0:T(8,128)} %param.13) | copy-start | bytes 196612
  3.6 14.9 %collective-permute-start = (bf16[576,128]{1,0:T(8,128)(2,1)S(1)}, bf16[576,128]{1,0:T(8,128)(2,1)S(1)}, u32[]{:S(2)}, u32[]{:S(2)}) collective-permute-start(bf16[576,128]{1,0:T(8,128)(2,1)S(1)} %get-tuple-element.14), channel_id=1, source_target_pairs={{0,16},{16,0},{1,17},{17,1},{2,18},{18,2},{3,19},{19,3},{4,20},{20... | collective-permute-start | bytes 442376 | tf_op jit(solution)/shard_map/ppermute | solution.py:591
  6.6 12.6 %collective-permute-start.1 = (bf16[512,128]{1,0:T(8,128)(2,1)S(1)}, bf16[512,128]{1,0:T(8,128)(2,1)S(1)}, u32[]{:S(2)}, u32[]{:S(2)}) collective-permute-start(bf16[512,128]{1,0:T(8,128)(2,1)S(1)} %get-tuple-element.15), channel_id=1, source_target_pairs={{0,16},{1,17},{2,18},{3,19},{4,20},{5,21},{6,22},{7,23},{8,24},{9,... | collective-permute-start | bytes 393224 | tf_op jit(solution)/shard_map/ppermute | solution.py:28
  8.7 8.3 %collective-permute-start.2 = (f32[3,4,128]{1,2,0:T(8,128)S(1)}, f32[3,4,128]{1,2,0:T(8,128)S(1)}, u32[]{:S(2)}, u32[]{:S(2)}) collective-permute-start(f32[3,4,128]{1,2,0:T(8,128)S(1)} %get-tuple-element.27), channel_id=1, source_target_pairs={{1,0},{2,1},{3,2},{5,4},{6,5},{7,6},{9,8},{10,9},{11,10},{13,12},{... | collective-permute-start | bytes 18440 | tf_op jit(solution)/shard_map/ppermute | solution.py:28
  10.0 8.2 %collective-permute-start.3 = (f32[3,4,128]{1,2,0:T(8,128)S(1)}, f32[3,4,128]{1,2,0:T(8,128)S(1)}, u32[]{:S(2)}, u32[]{:S(2)}) collective-permute-start(f32[3,4,128]{1,2,0:T(8,128)S(1)} %get-tuple-element.28), channel_id=1, source_target_pairs={{0,1},{1,2},{2,3},{4,5},{5,6},{6,7},{8,9},{9,10},{10,11},{12,13},{... | collective-permute-start | bytes 18440 | tf_op jit(solution)/shard_map/ppermute | solution.py:28
  18.6 0.7 copy-start.5
  19.2 0.9 %slice-start.1 = ((bf16[576,128]{1,0:T(8,128)(2,1)}), bf16[512,128]{1,0:T(8,128)(2,1)S(1)}, s32[]{:S(2)}) async-start(bf16[576,128]{1,0:T(8,128)(2,1)} %copy-done.5), calls=%async_computation.3 | async-start | bytes 262144 | tf_op jit(solution)/shard_map/slice | solution.py:605
  20.2 1.8 %slice-start = ((bf16[576,128]{1,0:T(8,128)(2,1)}), bf16[24,128]{1,0:T(8,128)(2,1)S(1)}, s32[]{:S(2)}) async-start(bf16[576,128]{1,0:T(8,128)(2,1)} %copy-done.5), calls=%async_computation.2 | async-start | bytes 12288 | tf_op jit(solution)/shard_map/slice | solution.py:602
  20.2 14.3 %collective-permute-start.4 = (bf16[1040,128]{1,0:T(8,128)(2,1)S(1)}, bf16[1040,128]{1,0:T(8,128)(2,1)S(1)}, u32[]{:S(2)}, u32[]{:S(2)}) collective-permute-start(bf16[1040,128]{1,0:T(8,128)(2,1)S(1)} %pad_maximum_fusion.3.refs_0_), channel_id=1, source_target_pairs={{0,4},{4,0},{8,12},{12,8},{1,5},{5,1},{9,13},{13,9},{2,6},{6,2},{1... | collective-permute-start | bytes 798728 | tf_op jit(solution)/shard_map/ppermute | solution.py:546
  20.2 8.8 %collective-permute-start.5 = (bf16[1040,128]{1,0:T(8,128)(2,1)S(1)}, bf16[1040,128]{1,0:T(8,128)(2,1)S(1)}, u32[]{:S(2)}, u32[]{:S(2)}) collective-permute-start(bf16[1040,128]{1,0:T(8,128)(2,1)S(1)} %pad_maximum_fusion.3.refs_0_), channel_id=1, source_target_pairs={{0,8},{4,12},{8,0},{12,4},{1,9},{5,13},{9,1},{13,5},{2,10},{6,14},... | collective-permute-start | bytes 798728 | tf_op jit(solution)/shard_map/ppermute | solution.py:546
  29.1 16.6 %collective-permute-start.6 = (bf16[1040,128]{1,0:T(8,128)(2,1)S(1)}, bf16[1040,128]{1,0:T(8,128)(2,1)S(1)}, u32[]{:S(2)}, u32[]{:S(2)}) collective-permute-start(bf16[1040,128]{1,0:T(8,128)(2,1)S(1)} %collective-permute-done.5.refs_2_), channel_id=1, source_target_pairs={{0,4},{4,0},{8,12},{12,8},{1,5},{5,1},{9,13},{13,9},{2,6},{6,2},{1... | collective-permute-start | bytes 798728 | tf_op jit(solution)/shard_map/ppermute | solution.py:546
  29.2 16.4 %collective-permute-start.7 = (bf16[544,128]{1,0:T(8,128)(2,1)S(1)}, bf16[544,128]{1,0:T(8,128)(2,1)S(1)}, u32[]{:S(2)}, u32[]{:S(2)}) collective-permute-start(bf16[544,128]{1,0:T(8,128)(2,1)S(1)} %maximum_maximum_fusion.1.refs_4_), channel_id=1, source_target_pairs={{0,1},{1,0},{2,3},{3,2},{4,5},{5,4},{6,7},{7,6},{8,9},{9,8},{10,11... | collective-permute-start | bytes 417800 | tf_op jit(solution)/shard_map/ppermute | solution.py:536
  31.7 13.9 %collective-permute-start.8 = (bf16[544,128]{1,0:T(8,128)(2,1)S(1)}, bf16[544,128]{1,0:T(8,128)(2,1)S(1)}, u32[]{:S(2)}, u32[]{:S(2)}) collective-permute-start(bf16[544,128]{1,0:T(8,128)(2,1)S(1)} %maximum_maximum_fusion.1.refs_4_), channel_id=1, source_target_pairs={{0,2},{1,3},{2,0},{3,1},{4,6},{5,7},{6,4},{7,5},{8,10},{9,11},{10,... | collective-permute-start | bytes 417800 | tf_op jit(solution)/shard_map/ppermute | solution.py:536
  34.5 11.1 %collective-permute-start.9 = (bf16[544,128]{1,0:T(8,128)(2,1)S(1)}, bf16[544,128]{1,0:T(8,128)(2,1)S(1)}, u32[]{:S(2)}, u32[]{:S(2)}) collective-permute-start(bf16[544,128]{1,0:T(8,128)(2,1)S(1)} %maximum_maximum_fusion.1.refs_4_), channel_id=1, source_target_pairs={{0,3},{1,2},{2,1},{3,0},{4,7},{5,6},{6,5},{7,4},{8,11},{9,10},{10,... | collective-permute-start | bytes 417800 | tf_op jit(solution)/shard_map/ppermute | solution.py:536
  34.5 11.0 %collective-permute-start.10 = (f32[3,136,128]{1,2,0:T(8,128)S(1)}, f32[3,136,128]{1,2,0:T(8,128)S(1)}, u32[]{:S(2)}, u32[]{:S(2)}) collective-permute-start(f32[3,136,128]{1,2,0:T(8,128)S(1)} %pad_maximum_fusion.2), channel_id=1, source_target_pairs={{0,16},{16,0},{1,17},{17,1},{2,18},{18,2},{3,19},{19,3},{4,20},{20... | collective-permute-start | bytes 626696 | tf_op jit(solution)/shard_map/ppermute | solution.py:631
  52.1 9.2 %all-to-all-start = ((f32[8,56,128]{2,1,0:T(8,128)}), f32[8,56,128]{2,1,0:T(8,128)S(1)}, u32[]{:S(2)}, u32[]{:S(2)}) async-start(f32[8,56,128]{2,1,0:T(8,128)} %bitcast.19), calls=%async_computation | async-start | bytes 458752 | tf_op jit(solution)/shard_map/all_to_all | solution.py:32
  62.1 12.2 %all-to-all-start.1 = ((f32[32,8,128]{2,1,0:T(8,128)}), f32[32,8,128]{2,1,0:T(8,128)S(1)}, u32[]{:S(2)}, u32[]{:S(2)}) async-start(f32[32,8,128]{2,1,0:T(8,128)} %combine.1), calls=%async_computation.1 | async-start | bytes 262144 | tf_op jit(solution)/shard_map/all_to_all | solution.py:32
